TPU v7x, 256 devices: a whole 4x4x8 slice. The times are simulated.
256 devices in a mesh: row: 4 (over x), col: 4 (over y), slab: 16 (over z, core).
Axes of the slice: x: 4, y: 4, z: 8, core: 2. Of those that a mesh axis runs over, the one named last changes fastest.
Arguments:
- a_tiles: float32 [2048, 27, 4096], P(('row', 'col', 'slab')), may hold values from -0.75 to 0.75
- p_tiles: float32 [2048, 4096], P(('row', 'col', 'slab')), may hold values from -0.75 to 0.75
- col_ids: int32 [2048, 27], P(('row', 'col', 'slab')), may hold values from 0 to 2047, as said below
- row_tiles: int32 [2048], P(('row', 'col', 'slab')), may hold values from 1 to 27
- agg_ids: int32 [4, 4, 128], P(None, 'col'), may hold values from 0 to 7
- owner_map: int32 [4, 16, 8], P('col', 'slab'), may hold values from 0 to 7, each once within a row
Outputs:
- coarse: float32 [4, 4, 16, 2, 64, 1536], P('row', 'col', 'slab')
Inputs may be any that keep to these rules, and one draw needn't show every extreme that they name: `col_ids`: slot 0 of each fine block names the block itself; every entry names a block with the same col index and a slab index that differs by at most 1. `owner_map`: each group's entries are a permutation.
All inputs are finite; a program needn't handle non-finite values.
Results may differ from a plain program's by a relative error of at most 0.0001.
Values sent between devices are 32-bit elements; how exact they have to be, the bound alone decides.
No kernel may reach another device: no remote copies, remote signals or barrier semaphores. Data moves between devices by JAX's collectives and lax.ppermute only.
A program may use at most 128 MiB of HBM per device.

v0:
```python
import functools

import jax
import jax.numpy as jnp
from jax import lax
from jax.experimental import pallas as pl
from jax.experimental.pallas import tpu as pltpu
from jax.sharding import PartitionSpec as P

B = 64
CW = 64
KT = 27
RB = 8
NPOOL = 8
N_ROW = 4
UNROLL = 8
TILES = RB * KT
PAIRS = NPOOL // 2
LIST = TILES + UNROLL
GROUP = 3
XP = 32
PLACES = ((0, 1), (4, 3), (5, 6), (2,), (7,))
f32 = jnp.float32
bf16 = jnp.bfloat16


def split(x):
    hi = x.astype(bf16)
    return hi, (x - hi.astype(f32)).astype(bf16)


def in_hbm(x):
    return pltpu.with_memory_space_constraint(x, pltpu.HBM)


def left_kernel(
    n_slab,
    a_hbm,
    p_hbm,
    cols_hbm,
    counts_hbm,
    aggs_hbm,
    owners_hbm,
    t_ref,
    todo,
    a_buf,
    p_in,
    p_buf,
    lhs_buf,
    cols,
    counts,
    aggs,
    owners,
    a_sem,
    sem,
):
    small = [
        pltpu.make_async_copy(source, target, sem.at[n])
        for n, (source, target) in enumerate(
            [
                (p_hbm, p_in),
                (cols_hbm, cols),
                (counts_hbm, counts),
                (aggs_hbm, aggs),
                (owners_hbm, owners),
            ]
        )
    ]
    rows = GROUP * XP * RB

    def fetch(n):
        part = pl.ds(n * rows, rows)
        return pltpu.make_async_copy(a_hbm.at[part], a_buf.at[part], a_sem.at[n])

    for copy in small:
        copy.start()
    for n in range(KT // GROUP):
        fetch(n).start()
    for copy in small:
        copy.wait()
    row = lax.axis_index("row")
    slab = lax.axis_index("slab")
    for x in range(XP):
        p_buf[pl.ds(x, RB, stride=XP), :] = p_in[:, x * 128 : (x + 1) * 128]
    first = lax.broadcasted_iota(jnp.int32, (XP, 128), 1) < 64
    first_out = lax.broadcasted_iota(jnp.int32, (CW, 128), 1) < 64
    places = []
    for i in range(RB):
        packed = p_buf[i * XP : (i + 1) * XP, :]
        own = jnp.concatenate([packed[:, :64], packed[:, 64:]], axis=0)
        hi, lo = split(own.T)
        lhs_buf[i] = jnp.concatenate([hi, hi, lo, lo], axis=1)
        position = owners[0, 0, aggs[row, 0, slab * RB + i]]
        places.append((((position >> 1) - row) & (N_ROW - 1)) * 2 + (position & 1))

    def group(n, lengths):
        fetch(n).wait()
        own_at, pair_at, far_at = lengths
        entries = []
        for i in range(RB):
            for u in range(GROUP):
                k = n * GROUP + u
                source = cols[i, k]
                source_slab = (source >> 3) & (n_slab - 1)
                entries.append(
                    (
                        (source << 8) + (k * RB + i + (places[i] << 19)),
                        source_slab == slab,
                        source_slab == slab ^ 1,
                        k < counts[i],
                    )
                )
        for entry, is_own, is_pair, live in entries:
            todo[jnp.where(is_own, own_at, jnp.where(is_pair, pair_at, far_at))] = entry
            one = live.astype(jnp.int32)
            own_one = jnp.where(is_own, one, 0)
            pair_one = jnp.where(is_pair, one, 0)
            own_at = own_at + own_one
            pair_at = pair_at + pair_one
            far_at = far_at + (one - own_one - pair_one)
        for i in range(RB):
            lhs = lhs_buf[i]
            parts = []
            for u in range(GROUP):
                k = n * GROUP + u
                a = a_buf[pl.ds(k * (XP * RB) + i, XP, stride=RB), :]
                turned = pltpu.roll(a, 64, 1)
                two = jnp.concatenate(
                    [jnp.where(first, a, turned), jnp.where(first, turned, a)], axis=0
                )
                hi, lo = split(two)
                parts.append(jnp.concatenate([hi, lo, hi, lo], axis=0))

            t = jnp.dot(
                lhs, jnp.concatenate(parts, axis=1), preferred_element_type=f32
            )
            for u in range(GROUP):
                one = t[:, u * 128 : (u + 1) * 128]
                rest = one - one.astype(bf16).astype(f32)
                t_ref[(n * GROUP + u) * RB + i] = jnp.where(
                    first_out, one, rest
                ).astype(bf16)
        return own_at, pair_at, far_at

    starts = tuple(jnp.int32(g * LIST) for g in range(3))
    ends = lax.fori_loop(0, KT // GROUP, group, starts)
    for g in range(3):
        for u in range(UNROLL):
            todo[ends[g] + u] = 8 << 19
        todo[3 * LIST + g] = ends[g] - starts[g]


def left_products(a_tiles, p_tiles, col_ids, row_tiles, agg_ids, owner_map):
    rows = a_tiles.transpose(1, 0, 2).reshape(KT, RB, XP, 128)
    rows = rows.transpose(0, 2, 1, 3).reshape(KT * XP * RB, 128)
    vmem = pl.BlockSpec(memory_space=pltpu.VMEM)
    smem = pl.BlockSpec(memory_space=pltpu.SMEM)
    hbm = pl.BlockSpec(memory_space=pltpu.HBM)
    return pl.pallas_call(
        functools.partial(left_kernel, lax.axis_size("slab")),
        out_shape=[
            jax.ShapeDtypeStruct((TILES, CW, 128), bf16),
            jax.ShapeDtypeStruct((3 * LIST + 3,), jnp.int32),
        ],
        in_specs=[hbm] * 6,
        out_specs=[vmem, smem],
        scratch_shapes=[
            pltpu.VMEM((KT * XP * RB, 128), f32),
            pltpu.VMEM((RB, B * CW), f32),
            pltpu.VMEM((RB * XP, 128), f32),
            pltpu.VMEM((RB, CW, 256), bf16),
            pltpu.SMEM(col_ids.shape, jnp.int32),
            pltpu.SMEM(row_tiles.shape, jnp.int32),
            pltpu.SMEM(agg_ids.shape, jnp.int32),
            pltpu.SMEM(owner_map.shape, jnp.int32),
            pltpu.SemaphoreType.DMA((KT // GROUP,)),
            pltpu.SemaphoreType.DMA((5,)),
        ],
        compiler_params=pltpu.CompilerParams(vmem_limit_bytes=24 << 20),
        cost_estimate=pl.CostEstimate(
            flops=4_000_000_000, bytes_accessed=8_000_000, transcendentals=0
        ),
        name="left_products",
    )(*map(in_hbm, (rows, p_tiles, col_ids, row_tiles, agg_ids, owner_map)))


def right_kernel(which, sizes, n_after, *refs):
    n_slab, row_shift = sizes
    todo, aggs, t_ref, p_ref = refs[:4]
    refs = refs[4 + n_after :]
    outs = refs[: len(PLACES)]
    flat, panel, acc = refs[len(PLACES) :]
    row = lax.axis_index("row")
    slab = lax.axis_index("slab")
    if which == 0:
        near_slab = slab
    elif which == 1:
        near_slab = slab ^ 1
    else:
        near_slab = jnp.clip(slab + 2 * (slab & 1) - 1, 0, n_slab - 1)
    left = lax.broadcasted_iota(jnp.int32, (RB, 128), 1) < 64
    sub = lax.broadcasted_iota(jnp.int32, (RB, 128), 0)
    for b in range(N_ROW):
        near_row = (row + b) & (N_ROW - 1)
        odd = jnp.zeros((RB, 128), jnp.int32)
        for i in range(RB):
            odd = jnp.where(sub == i, aggs[near_row, 0, near_slab * RB + i], odd)
        odd = (odd & 1) == 1
        keep_even = jnp.logical_and(left, jnp.logical_not(odd))
        keep_odd = jnp.logical_and(jnp.logical_not(left), odd)
        for y in range(0, B, 2):
            v = p_ref[b * RB : (b + 1) * RB, y * 64 : y * 64 + 128]
            w = pltpu.roll(v, 64, 1)
            zero = jnp.zeros_like(v)
            flat[pl.ds(b * RB * B + y, RB, stride=B), :] = jnp.where(
                keep_even, v, jnp.where(keep_odd, w, zero)
            )
            flat[pl.ds(b * RB * B + y + 1, RB, stride=B), :] = jnp.where(
                keep_odd, v, jnp.where(keep_even, w, zero)
            )

    def prepare(m, carry):
        hi, lo = split(flat[pl.ds(pl.multiple_of(m * B, B), B), :])
        panel[m, :, :128] = hi
        panel[m, :, 128:] = lo
        return carry

    lax.fori_loop(0, N_ROW * RB, prepare, 0, unroll=4)
    acc[: 8 * PAIRS] = jnp.zeros((8 * PAIRS, CW, 128), f32)

    def step(n, carry):
        for u in range(UNROLL):
            entry = todo[which * LIST + n * UNROLL + u]
            source = (entry >> 8) & 2047
            source_row = source >> row_shift
            source_block = source & (RB - 1)
            source_slab = (source >> 3) & (n_slab - 1)
            pair = aggs[source_row, 0, source_slab * RB + source_block] >> 1
            at = ((source_row - row) & (N_ROW - 1)) * RB + source_block
            w = panel[at]
            o = jnp.dot(
                t_ref[entry & 255],
                jnp.concatenate([w, w], axis=0),
                preferred_element_type=f32,
            )
            acc[(entry >> 19) * PAIRS + pair] += o[:, :128] + o[:, 128:]
        return carry

    lax.fori_loop(0, (todo[3 * LIST + which] + UNROLL - 1) // UNROLL, step, 0)
    for out, places in zip(outs, PLACES, strict=True):
        for n, place in enumerate(places):
            out[n] = acc[place * PAIRS : (place + 1) * PAIRS]


def right_products(which, todo, agg_ids, t, panel, after=()):
    n_slab = lax.axis_size("slab")
    sizes = (n_slab, (RB * n_slab * lax.axis_size("col")).bit_length() - 1)
    vmem = pl.BlockSpec(memory_space=pltpu.VMEM)
    smem = pl.BlockSpec(memory_space=pltpu.SMEM)
    anywhere = pl.BlockSpec(memory_space=pl.ANY)
    return pl.pallas_call(
        functools.partial(right_kernel, which, sizes, len(after)),
        out_shape=[
            jax.ShapeDtypeStruct((len(places), PAIRS, CW, 128), f32)
            for places in PLACES
        ],
        in_specs=[smem, smem, vmem, vmem] + [anywhere] * len(after),
        out_specs=[vmem] * len(PLACES),
        scratch_shapes=[
            pltpu.VMEM((N_ROW * RB * B, 128), f32),
            pltpu.VMEM((N_ROW * RB, B, 256), bf16),
            pltpu.VMEM((9 * PAIRS, CW, 128), f32),
        ],
        compiler_params=pltpu.CompilerParams(vmem_limit_bytes=16 << 20),
        cost_estimate=pl.CostEstimate(
            flops=3_000_000_000, bytes_accessed=5_000_000, transcendentals=0
        ),
        name="right_products",
    )(todo, agg_ids, t, panel, *after)


def add_kernel(up_two, up_one, down_two, down_one, *refs):
    refs[-2][0] = up_two[0] + up_one[0]
    refs[-1][0] = down_two[0] + down_one[0]


def add_shares(up_two, up_one, down_two, down_one, after=()):
    vmem = pl.BlockSpec(memory_space=pltpu.VMEM)
    anywhere = pl.BlockSpec(memory_space=pl.ANY)
    return pl.pallas_call(
        add_kernel,
        out_shape=[jax.ShapeDtypeStruct((1, PAIRS, CW, 128), f32)] * 2,
        in_specs=[vmem] * 4 + [anywhere] * len(after),
        out_specs=[vmem] * 2,
        compiler_params=pltpu.CompilerParams(vmem_limit_bytes=2 << 20),
        name="add_shares",
    )(up_two, up_one, down_two, down_one, *after)


def finish_kernel(*refs):
    out = refs[-1]
    pair_is_upper = (lax.axis_index("slab") & 1) == 0
    upper, lower = 2 * PAIRS, 0
    firsts = [
        PAIRS,
        jnp.where(pair_is_upper, upper, lower),
        jnp.where(pair_is_upper, lower, upper),
    ]
    for g, first in enumerate(firsts):
        own, up_one, down_one, up_two, down_two = refs[5 * g : 5 * g + 5]
        for q in range(PAIRS):
            columns = pl.ds(pl.multiple_of((first + q) * 128, 128), 128)
            out[0, :, columns] = own[0, q] + down_one[1, q] + up_two[0, q]
            out[1, :, columns] = own[1, q] + up_one[1, q] + down_two[0, q]


def finish(parts):
    vmem = pl.BlockSpec(memory_space=pltpu.VMEM)
    return pl.pallas_call(
        finish_kernel,
        out_shape=jax.ShapeDtypeStruct((2, CW, 24 * CW), f32),
        in_specs=[vmem] * 15,
        out_specs=vmem,
        compiler_params=pltpu.CompilerParams(vmem_limit_bytes=24 << 20),
        name="finish",
    )(*parts)


def stack_kernel(*refs):
    out = refs[-1]
    for n, ref in enumerate(refs[:N_ROW]):
        out[n * RB : (n + 1) * RB, :] = ref[...]


def stack(blocks, after):
    vmem = pl.BlockSpec(memory_space=pltpu.VMEM)
    return pl.pallas_call(
        stack_kernel,
        out_shape=jax.ShapeDtypeStruct((N_ROW * RB, B * CW), f32),
        in_specs=[vmem] * N_ROW + [pl.BlockSpec(memory_space=pl.ANY)],
        out_specs=vmem,
        compiler_params=pltpu.CompilerParams(vmem_limit_bytes=2 << 20),
        name="stack",
    )(*blocks, after)


def on_device(a_tiles, p_tiles, col_ids, row_tiles, agg_ids, owner_map):
    n_slab = lax.axis_size("slab")
    ring = lambda step: [(i, (i + step) % N_ROW) for i in range(N_ROW)]
    twins = [(i, i ^ 1) for i in range(n_slab)]
    others = [
        (i, i + 2 * (i & 1) - 1)
        for i in range(n_slab)
        if 0 <= i + 2 * (i & 1) - 1 < n_slab
    ]
    up = lambda x: lax.ppermute(x, "row", ring(1))
    down = lambda x: lax.ppermute(x, "row", ring(-1))

    from_far = lax.ppermute(p_tiles, "row", ring(2))
    from_below = up(p_tiles)
    from_above = down(p_tiles)
    mid_blocks = [p_tiles, from_above, from_far, from_below]
    t, todo = left_products(
        a_tiles, p_tiles, col_ids, row_tiles, agg_ids, owner_map
    )
    stacked = stack(mid_blocks, todo)
    from_other = lax.ppermute(stacked, "slab", others)
    from_twin = lax.ppermute(stacked, "slab", twins)

    own = right_products(0, todo, agg_ids, t, stacked)
    own_up, own_down = up(own[1]), down(own[2])
    twin = right_products(1, todo, agg_ids, t, from_twin, (own[0],))
    twin_up, twin_down = up(twin[1]), down(twin[2])
    own_sums = add_shares(own[3], own_up, own[4], own_down, (twin[0],))
    own_two = up(own_sums[0]), down(own_sums[1])
    other = right_products(
        2, todo, agg_ids, t, from_other, (twin[0], own_sums[0])
    )
    other_up, other_down = up(other[1]), down(other[2])
    twin_sums = add_shares(twin[3], twin_up, twin[4], twin_down, (other[0],))
    twin_two = up(twin_sums[0]), down(twin_sums[1])
    other_sums = add_shares(
        other[3], other_up, other[4], other_down, (twin_sums[0],)
    )
    other_two = up(other_sums[0]), down(other_sums[1])
    out = finish(
        [own[0], own_up, own_down, *own_two]
        + [twin[0], twin_up, twin_down, *twin_two]
        + [other[0], other_up, other_down, *other_two]
    )
    return out.reshape(1, 1, 1, 2, CW, 24 * CW)


def solution(mesh):
    placed = (
        P(("row", "col", "slab"), None, None),
        P(("row", "col", "slab"), None),
        P(("row", "col", "slab"), None),
        P(("row", "col", "slab")),
        P(None, "col", None),
        P("col", "slab", None),
    )
    return jax.shard_map(
        on_device,
        mesh=mesh,
        in_specs=placed,
        out_specs=P("row", "col", "slab", None, None, None),
        check_vma=False,
    )
```

profile of v0, /device:TPU:136, one launch (start us, length us, event | category | flops | bytes accessed | tf_op | source)
XLA Modules:
  0.0 55.3 jit_solution(16356988593727612134)
XLA Ops:
  0.0 3.0 %collective-permute-start.1 = (f32[8,4096]{1,0:T(8,128)}, f32[8,4096]{1,0:T(8,128)S(1)}, u32[]{:S(2)}, u32[]{:S(2)}) collective-permute-start(f32[8,4096]{1,0:T(8,128)} %refs_0_.1), channel_id=1, source_target_pairs={{0,128},{64,192},{128,0},{192,64},{1,129},{65,193},{129,1},{193,65... | collective-permute-start | bytes 393224 | tf_op jit(solution)/shard_map/ppermute | solution.py:359
  3.0 1.1 %collective-permute-start = (f32[8,4096]{1,0:T(8,128)}, f32[8,4096]{1,0:T(8,128)S(1)}, u32[]{:S(2)}, u32[]{:S(2)}) collective-permute-start(f32[8,4096]{1,0:T(8,128)} %refs_0_.1), channel_id=1, source_target_pairs={{0,192},{64,0},{128,64},{192,128},{1,193},{65,1},{129,65},{193,129... | collective-permute-start | bytes 393224 | tf_op jit(solution)/shard_map/ppermute | solution.py:357
  4.2 0.9 %collective-permute-start.2 = (f32[8,4096]{1,0:T(8,128)}, f32[8,4096]{1,0:T(8,128)S(1)}, u32[]{:S(2)}, u32[]{:S(2)}) collective-permute-start(f32[8,4096]{1,0:T(8,128)} %refs_0_.1), channel_id=1, source_target_pairs={{0,64},{64,128},{128,192},{192,0},{1,65},{65,129},{129,193},{193,1... | collective-permute-start | bytes 393224 | tf_op jit(solution)/shard_map/ppermute | solution.py:356
  5.1 8.5 %left_products.1 = (bf16[216,64,128]{2,1,0:T(8,128)(2,1)S(1)}, s32[675]{0:T(1024)S(1)}) custom-call(f32[6912,128]{1,0:T(8,128)} %bitcast.8, f32[8,4096]{1,0:T(8,128)} %refs_0_.1, s32[8,27]{1,0:T(8,128)} %cols_hbm.1, s32[8]{0:T(128)} %counts_hbm.1, s32[4,1,128]{2,1,0:T(1,128)} %refs_1_.5, s32[1,1,8]{2,1,0:T(1,128)} %owners_hbm.1), custom_call_target="tpu_custom_call" | custom-call | flops 4000000000 | bytes 8000000 | tf_op jit(solution)/shard_map/left_products/pallas_call | solution.py:159
  13.6 0.0 collective-permute-done.1.refs_2_
  13.7 0.1 collective-permute-start.5
  13.8 2.1 %collective-permute-start.10 = (f32[32,4096]{1,0:T(8,128)S(1)}, f32[32,4096]{1,0:T(8,128)S(1)}, u32[]{:S(2)}, u32[]{:S(2)}) collective-permute-start(f32[32,4096]{1,0:T(8,128)S(1)} %stack.1.refs_3_), channel_id=1, source_target_pairs={{1,2},{2,1},{3,4},{4,3},{5,6},{6,5},{7,8},{8,7},{9,10},{10,9},{11,... | collective-permute-start | bytes 1572872 | tf_op jit(solution)/shard_map/ppermute | solution.py:367
  15.9 3.0 %right_products.3 = (f32[2,4,64,128]{3,2,1,0:T(8,128)S(1)}, f32[2,4,64,128]{3,2,1,0:T(8,128)S(1)}, f32[2,4,64,128]{3,2,1,0:T(8,128)S(1)}, f32[1,4,64,128]{3,2,1,0:T(8,128)S(1)}, f32[1,4,64,128]{3,2,1,0:T(8,128)S(1)}) custom-call(s32[675]{0:T(1024)S(1)} %get-tuple-element.28.refs_4_.refs_0_, s32[4,1,128]{2,1,0:T(1,128)S(1)} %copy-done.1, ...), custom_call_target="tpu_custom_call" | custom-call | flops 3000000000 | bytes 5000000 | tf_op jit(solution)/shard_map/right_products/pallas_call | solution.py:261
  18.9 0.7 %collective-permute-start.3 = (f32[2,4,64,128]{3,2,1,0:T(8,128)S(1)}, f32[2,4,64,128]{3,2,1,0:T(8,128)S(1)}, u32[]{:S(2)}, u32[]{:S(2)}) collective-permute-start(f32[2,4,64,128]{3,2,1,0:T(8,128)S(1)} %get-tuple-element.31), channel_id=1, source_target_pairs={{0,64},{64,128},{128,192},{192,0},{1,65},{65,129},{129,193},{193,1... | collective-permute-start | bytes 786440 | tf_op jit(solution)/shard_map/ppermute | solution.py:356
  19.6 2.6 %collective-permute-start.4 = (f32[2,4,64,128]{3,2,1,0:T(8,128)S(1)}, f32[2,4,64,128]{3,2,1,0:T(8,128)S(1)}, u32[]{:S(2)}, u32[]{:S(2)}) collective-permute-start(f32[2,4,64,128]{3,2,1,0:T(8,128)S(1)} %get-tuple-element.32), channel_id=1, source_target_pairs={{0,192},{64,0},{128,64},{192,128},{1,193},{65,1},{129,65},{193,129... | collective-permute-start | bytes 786440 | tf_op jit(solution)/shard_map/ppermute | solution.py:357
  22.3 0.0 collective-permute-done.5.refs_3_
  22.3 3.3 %right_products.4 = (f32[2,4,64,128]{3,2,1,0:T(8,128)S(1)}, f32[2,4,64,128]{3,2,1,0:T(8,128)S(1)}, f32[2,4,64,128]{3,2,1,0:T(8,128)S(1)}, f32[1,4,64,128]{3,2,1,0:T(8,128)S(1)}, f32[1,4,64,128]{3,2,1,0:T(8,128)S(1)}) custom-call(s32[675]{0:T(1024)S(1)} %get-tuple-element.28.refs_4_.refs_0_, s32[4,1,128]{2,1,0:T(1,128)S(1)} %copy-done.1, ...), custom_call_target="tpu_custom_call" | custom-call | flops 3000000000 | bytes 5000000 | tf_op jit(solution)/shard_map/right_products/pallas_call | solution.py:261
  25.5 0.1 collective-permute-start.8
  25.6 3.2 %collective-permute-start.9 = (f32[2,4,64,128]{3,2,1,0:T(8,128)S(1)}, f32[2,4,64,128]{3,2,1,0:T(8,128)S(1)}, u32[]{:S(2)}, u32[]{:S(2)}) collective-permute-start(f32[2,4,64,128]{3,2,1,0:T(8,128)S(1)} %get-tuple-element.39), channel_id=1, source_target_pairs={{0,192},{64,0},{128,64},{192,128},{1,193},{65,1},{129,65},{193,129... | collective-permute-start | bytes 786440 | tf_op jit(solution)/shard_map/ppermute | solution.py:357
  28.9 0.3 collective-permute-done.3.up_one.refs_1_
  29.1 0.0 collective-permute-done.4.down_one.refs_2_
  29.2 3.0 %right_products.5 = (f32[2,4,64,128]{3,2,1,0:T(8,128)S(1)}, f32[2,4,64,128]{3,2,1,0:T(8,128)S(1)}, f32[2,4,64,128]{3,2,1,0:T(8,128)S(1)}, f32[1,4,64,128]{3,2,1,0:T(8,128)S(1)}, f32[1,4,64,128]{3,2,1,0:T(8,128)S(1)}) custom-call(s32[675]{0:T(1024)S(1)} %get-tuple-element.28.refs_4_.refs_0_, s32[4,1,128]{2,1,0:T(1,128)S(1)} %copy-done.1, ...), custom_call_target="tpu_custom_call" | custom-call | flops 3000000000 | bytes 5000000 | tf_op jit(solution)/shard_map/right_products/pallas_call | solution.py:261
  32.2 0.9 %collective-permute-start.13 = (f32[2,4,64,128]{3,2,1,0:T(8,128)S(1)}, f32[2,4,64,128]{3,2,1,0:T(8,128)S(1)}, u32[]{:S(2)}, u32[]{:S(2)}) collective-permute-start(f32[2,4,64,128]{3,2,1,0:T(8,128)S(1)} %get-tuple-element.45), channel_id=1, source_target_pairs={{0,64},{64,128},{128,192},{192,0},{1,65},{65,129},{129,193},{193,1... | collective-permute-start | bytes 786440 | tf_op jit(solution)/shard_map/ppermute | solution.py:356
  33.1 2.4 %collective-permute-start.14 = (f32[2,4,64,128]{3,2,1,0:T(8,128)S(1)}, f32[2,4,64,128]{3,2,1,0:T(8,128)S(1)}, u32[]{:S(2)}, u32[]{:S(2)}) collective-permute-start(f32[2,4,64,128]{3,2,1,0:T(8,128)S(1)} %get-tuple-element.46), channel_id=1, source_target_pairs={{0,192},{64,0},{128,64},{192,128},{1,193},{65,1},{129,65},{193,129... | collective-permute-start | bytes 786440 | tf_op jit(solution)/shard_map/ppermute | solution.py:357
  35.6 1.5 %collective-permute-start.7 = (f32[1,4,64,128]{3,2,1,0:T(8,128)S(1)}, f32[1,4,64,128]{3,2,1,0:T(8,128)S(1)}, u32[]{:S(2)}, u32[]{:S(2)}) collective-permute-start(f32[1,4,64,128]{3,2,1,0:T(8,128)S(1)} %get-tuple-element.37), channel_id=1, source_target_pairs={{0,192},{64,0},{128,64},{192,128},{1,193},{65,1},{129,65},{193,129... | collective-permute-start | bytes 393224 | tf_op jit(solution)/shard_map/ppermute | solution.py:357
  37.1 0.0 collective-permute-done.8.up_one.refs_6_
  37.1 0.5 collective-permute-start.6
  37.6 0.0 collective-permute-done.9.down_one.refs_7_
  37.6 5.1 %collective-permute-done.13.up_one.refs_11_ = f32[2,4,64,128]{3,2,1,0:T(8,128)S(1)} collective-permute-done((f32[2,4,64,128]{3,2,1,0:T(8,128)S(1)}, f32[2,4,64,128]{3,2,1,0:T(8,128)S(1)}, u32[]{:S(2)}, u32[]{:S(2)}) %collective-permute-start.13) | collective-permute-done | bytes 262176 | tf_op jit(solution)/shard_map/ppermute | solution.py:356
  42.7 1.2 %collective-permute-start.15 = (f32[1,4,64,128]{3,2,1,0:T(8,128)S(1)}, f32[1,4,64,128]{3,2,1,0:T(8,128)S(1)}, u32[]{:S(2)}, u32[]{:S(2)}) collective-permute-start(f32[1,4,64,128]{3,2,1,0:T(8,128)S(1)} %get-tuple-element.49), channel_id=1, source_target_pairs={{0,64},{64,128},{128,192},{192,0},{1,65},{65,129},{129,193},{193,1... | collective-permute-start | bytes 393224 | tf_op jit(solution)/shard_map/ppermute | solution.py:356
  43.9 2.3 %collective-permute-start.16 = (f32[1,4,64,128]{3,2,1,0:T(8,128)S(1)}, f32[1,4,64,128]{3,2,1,0:T(8,128)S(1)}, u32[]{:S(2)}, u32[]{:S(2)}) collective-permute-start(f32[1,4,64,128]{3,2,1,0:T(8,128)S(1)} %get-tuple-element.50), channel_id=1, source_target_pairs={{0,192},{64,0},{128,64},{192,128},{1,193},{65,1},{129,65},{193,129... | collective-permute-start | bytes 393224 | tf_op jit(solution)/shard_map/ppermute | solution.py:357
  46.2 2.0 %collective-permute-start.12 = (f32[1,4,64,128]{3,2,1,0:T(8,128)S(1)}, f32[1,4,64,128]{3,2,1,0:T(8,128)S(1)}, u32[]{:S(2)}, u32[]{:S(2)}) collective-permute-start(f32[1,4,64,128]{3,2,1,0:T(8,128)S(1)} %get-tuple-element.44), channel_id=1, source_target_pairs={{0,192},{64,0},{128,64},{192,128},{1,193},{65,1},{129,65},{193,129... | collective-permute-start | bytes 393224 | tf_op jit(solution)/shard_map/ppermute | solution.py:357
  48.1 0.1 collective-permute-start.11
  48.2 1.1 %collective-permute-done.15.refs_13_ = f32[1,4,64,128]{3,2,1,0:T(8,128)S(1)} collective-permute-done((f32[1,4,64,128]{3,2,1,0:T(8,128)S(1)}, f32[1,4,64,128]{3,2,1,0:T(8,128)S(1)}, u32[]{:S(2)}, u32[]{:S(2)}) %collective-permute-start.15) | collective-permute-done | bytes 131104 | tf_op jit(solution)/shard_map/ppermute | solution.py:356
  49.3 1.9 %collective-permute-done.12.refs_9_ = f32[1,4,64,128]{3,2,1,0:T(8,128)S(1)} collective-permute-done((f32[1,4,64,128]{3,2,1,0:T(8,128)S(1)}, f32[1,4,64,128]{3,2,1,0:T(8,128)S(1)}, u32[]{:S(2)}, u32[]{:S(2)}) %collective-permute-start.12) | collective-permute-done | bytes 131104 | tf_op jit(solution)/shard_map/ppermute | solution.py:357
  51.1 3.2 %collective-permute-done.11.refs_8_ = f32[1,4,64,128]{3,2,1,0:T(8,128)S(1)} collective-permute-done((f32[1,4,64,128]{3,2,1,0:T(8,128)S(1)}, f32[1,4,64,128]{3,2,1,0:T(8,128)S(1)}, u32[]{:S(2)}, u32[]{:S(2)}) %collective-permute-start.11) | collective-permute-done | bytes 131104 | tf_op jit(solution)/shard_map/ppermute | solution.py:356
  54.3 1.0 %finish.1 = f32[2,64,1536]{2,1,0:T(8,128)} custom-call(f32[2,4,64,128]{3,2,1,0:T(8,128)S(1)} %get-tuple-element.30.refs_4_.refs_0_, f32[2,4,64,128]{3,2,1,0:T(8,128)S(1)} %collective-permute-done.3.up_one.refs_1_, f32[2,4,64,128]{3,2,1,0:T(8,128)S(1)} %collective-permute-done.4.down_one.refs_2_, f32[1,4,64,128]{3,2,1,0:T(8,128)S(1)} %collective-permute-done.6.refs_3_, ...), custom_call_target="tpu_custom_call" | custom-call | tf_op jit(solution)/shard_map/finish/pallas_call | solution.py:319
  (15 shorter events, 0.2 us)
Async XLA Ops:
  0.0 13.6 %collective-permute-start.1 = (f32[8,4096]{1,0:T(8,128)}, f32[8,4096]{1,0:T(8,128)S(1)}, u32[]{:S(2)}, u32[]{:S(2)}) collective-permute-start(f32[8,4096]{1,0:T(8,128)} %refs_0_.1), channel_id=1, source_target_pairs={{0,128},{64,192},{128,0},{192,64},{1,129},{65,193},{129,1},{193,65... | collective-permute-start | bytes 393224 | tf_op jit(solution)/shard_map/ppermute | solution.py:359
  3.0 10.6 %collective-permute-start = (f32[8,4096]{1,0:T(8,128)}, f32[8,4096]{1,0:T(8,128)S(1)}, u32[]{:S(2)}, u32[]{:S(2)}) collective-permute-start(f32[8,4096]{1,0:T(8,128)} %refs_0_.1), channel_id=1, source_target_pairs={{0,192},{64,0},{128,64},{192,128},{1,193},{65,1},{129,65},{193,129... | collective-permute-start | bytes 393224 | tf_op jit(solution)/shard_map/ppermute | solution.py:357
  4.2 9.5 %collective-permute-start.2 = (f32[8,4096]{1,0:T(8,128)}, f32[8,4096]{1,0:T(8,128)S(1)}, u32[]{:S(2)}, u32[]{:S(2)}) collective-permute-start(f32[8,4096]{1,0:T(8,128)} %refs_0_.1), channel_id=1, source_target_pairs={{0,64},{64,128},{128,192},{192,0},{1,65},{65,129},{129,193},{193,1... | collective-permute-start | bytes 393224 | tf_op jit(solution)/shard_map/ppermute | solution.py:356
  5.1 8.6 %copy-start = (f32[8,4096]{1,0:T(8,128)S(1)}, f32[8,4096]{1,0:T(8,128)}, u32[]{:S(2)}) copy-start(f32[8,4096]{1,0:T(8,128)} %refs_0_.1) | copy-start | bytes 393220
  5.1 10.9 %copy-start.1 = (s32[4,1,128]{2,1,0:T(1,128)S(1)}, s32[4,1,128]{2,1,0:T(1,128)}, u32[]{:S(2)}) copy-start(s32[4,1,128]{2,1,0:T(1,128)} %refs_1_.5) | copy-start | bytes 6148
  13.7 8.6 %collective-permute-start.5 = (f32[32,4096]{1,0:T(8,128)S(1)}, f32[32,4096]{1,0:T(8,128)S(1)}, u32[]{:S(2)}, u32[]{:S(2)}) collective-permute-start(f32[32,4096]{1,0:T(8,128)S(1)} %stack.1.refs_3_), channel_id=1, source_target_pairs={{0,1},{1,0},{2,3},{3,2},{4,5},{5,4},{6,7},{7,6},{8,9},{9,8},{10,11... | collective-permute-start | bytes 1572872 | tf_op jit(solution)/shard_map/ppermute | solution.py:368
  13.8 15.4 %collective-permute-start.10 = (f32[32,4096]{1,0:T(8,128)S(1)}, f32[32,4096]{1,0:T(8,128)S(1)}, u32[]{:S(2)}, u32[]{:S(2)}) collective-permute-start(f32[32,4096]{1,0:T(8,128)S(1)} %stack.1.refs_3_), channel_id=1, source_target_pairs={{1,2},{2,1},{3,4},{4,3},{5,6},{6,5},{7,8},{8,7},{9,10},{10,9},{11,... | collective-permute-start | bytes 1572872 | tf_op jit(solution)/shard_map/ppermute | solution.py:367
  18.9 10.2 %collective-permute-start.3 = (f32[2,4,64,128]{3,2,1,0:T(8,128)S(1)}, f32[2,4,64,128]{3,2,1,0:T(8,128)S(1)}, u32[]{:S(2)}, u32[]{:S(2)}) collective-permute-start(f32[2,4,64,128]{3,2,1,0:T(8,128)S(1)} %get-tuple-element.31), channel_id=1, source_target_pairs={{0,64},{64,128},{128,192},{192,0},{1,65},{65,129},{129,193},{193,1... | collective-permute-start | bytes 786440 | tf_op jit(solution)/shard_map/ppermute | solution.py:356
  19.6 9.5 %collective-permute-start.4 = (f32[2,4,64,128]{3,2,1,0:T(8,128)S(1)}, f32[2,4,64,128]{3,2,1,0:T(8,128)S(1)}, u32[]{:S(2)}, u32[]{:S(2)}) collective-permute-start(f32[2,4,64,128]{3,2,1,0:T(8,128)S(1)} %get-tuple-element.32), channel_id=1, source_target_pairs={{0,192},{64,0},{128,64},{192,128},{1,193},{65,1},{129,65},{193,129... | collective-permute-start | bytes 786440 | tf_op jit(solution)/shard_map/ppermute | solution.py:357
  25.5 11.5 %collective-permute-start.8 = (f32[2,4,64,128]{3,2,1,0:T(8,128)S(1)}, f32[2,4,64,128]{3,2,1,0:T(8,128)S(1)}, u32[]{:S(2)}, u32[]{:S(2)}) collective-permute-start(f32[2,4,64,128]{3,2,1,0:T(8,128)S(1)} %get-tuple-element.38), channel_id=1, source_target_pairs={{0,64},{64,128},{128,192},{192,0},{1,65},{65,129},{129,193},{193,1... | collective-permute-start | bytes 786440 | tf_op jit(solution)/shard_map/ppermute | solution.py:356
  25.6 12.0 %collective-permute-start.9 = (f32[2,4,64,128]{3,2,1,0:T(8,128)S(1)}, f32[2,4,64,128]{3,2,1,0:T(8,128)S(1)}, u32[]{:S(2)}, u32[]{:S(2)}) collective-permute-start(f32[2,4,64,128]{3,2,1,0:T(8,128)S(1)} %get-tuple-element.39), channel_id=1, source_target_pairs={{0,192},{64,0},{128,64},{192,128},{1,193},{65,1},{129,65},{193,129... | collective-permute-start | bytes 786440 | tf_op jit(solution)/shard_map/ppermute | solution.py:357
  32.2 10.5 %collective-permute-start.13 = (f32[2,4,64,128]{3,2,1,0:T(8,128)S(1)}, f32[2,4,64,128]{3,2,1,0:T(8,128)S(1)}, u32[]{:S(2)}, u32[]{:S(2)}) collective-permute-start(f32[2,4,64,128]{3,2,1,0:T(8,128)S(1)} %get-tuple-element.45), channel_id=1, source_target_pairs={{0,64},{64,128},{128,192},{192,0},{1,65},{65,129},{129,193},{193,1... | collective-permute-start | bytes 786440 | tf_op jit(solution)/shard_map/ppermute | solution.py:356
  33.1 9.6 %collective-permute-start.14 = (f32[2,4,64,128]{3,2,1,0:T(8,128)S(1)}, f32[2,4,64,128]{3,2,1,0:T(8,128)S(1)}, u32[]{:S(2)}, u32[]{:S(2)}) collective-permute-start(f32[2,4,64,128]{3,2,1,0:T(8,128)S(1)} %get-tuple-element.46), channel_id=1, source_target_pairs={{0,192},{64,0},{128,64},{192,128},{1,193},{65,1},{129,65},{193,129... | collective-permute-start | bytes 786440 | tf_op jit(solution)/shard_map/ppermute | solution.py:357
  35.6 12.6 %collective-permute-start.7 = (f32[1,4,64,128]{3,2,1,0:T(8,128)S(1)}, f32[1,4,64,128]{3,2,1,0:T(8,128)S(1)}, u32[]{:S(2)}, u32[]{:S(2)}) collective-permute-start(f32[1,4,64,128]{3,2,1,0:T(8,128)S(1)} %get-tuple-element.37), channel_id=1, source_target_pairs={{0,192},{64,0},{128,64},{192,128},{1,193},{65,1},{129,65},{193,129... | collective-permute-start | bytes 393224 | tf_op jit(solution)/shard_map/ppermute | solution.py:357
  37.1 11.1 %collective-permute-start.6 = (f32[1,4,64,128]{3,2,1,0:T(8,128)S(1)}, f32[1,4,64,128]{3,2,1,0:T(8,128)S(1)}, u32[]{:S(2)}, u32[]{:S(2)}) collective-permute-start(f32[1,4,64,128]{3,2,1,0:T(8,128)S(1)} %get-tuple-element.36.refs_5_), channel_id=1, source_target_pairs={{0,64},{64,128},{128,192},{192,0},{1,65},{65,129},{129,193},{193,1... | collective-permute-start | bytes 393224 | tf_op jit(solution)/shard_map/ppermute | solution.py:356
  42.7 6.5 %collective-permute-start.15 = (f32[1,4,64,128]{3,2,1,0:T(8,128)S(1)}, f32[1,4,64,128]{3,2,1,0:T(8,128)S(1)}, u32[]{:S(2)}, u32[]{:S(2)}) collective-permute-start(f32[1,4,64,128]{3,2,1,0:T(8,128)S(1)} %get-tuple-element.49), channel_id=1, source_target_pairs={{0,64},{64,128},{128,192},{192,0},{1,65},{65,129},{129,193},{193,1... | collective-permute-start | bytes 393224 | tf_op jit(solution)/shard_map/ppermute | solution.py:356
  43.9 5.4 %collective-permute-start.16 = (f32[1,4,64,128]{3,2,1,0:T(8,128)S(1)}, f32[1,4,64,128]{3,2,1,0:T(8,128)S(1)}, u32[]{:S(2)}, u32[]{:S(2)}) collective-permute-start(f32[1,4,64,128]{3,2,1,0:T(8,128)S(1)} %get-tuple-element.50), channel_id=1, source_target_pairs={{0,192},{64,0},{128,64},{192,128},{1,193},{65,1},{129,65},{193,129... | collective-permute-start | bytes 393224 | tf_op jit(solution)/shard_map/ppermute | solution.py:357
  46.2 5.0 %collective-permute-start.12 = (f32[1,4,64,128]{3,2,1,0:T(8,128)S(1)}, f32[1,4,64,128]{3,2,1,0:T(8,128)S(1)}, u32[]{:S(2)}, u32[]{:S(2)}) collective-permute-start(f32[1,4,64,128]{3,2,1,0:T(8,128)S(1)} %get-tuple-element.44), channel_id=1, source_target_pairs={{0,192},{64,0},{128,64},{192,128},{1,193},{65,1},{129,65},{193,129... | collective-permute-start | bytes 393224 | tf_op jit(solution)/shard_map/ppermute | solution.py:357
  48.1 6.2 %collective-permute-start.11 = (f32[1,4,64,128]{3,2,1,0:T(8,128)S(1)}, f32[1,4,64,128]{3,2,1,0:T(8,128)S(1)}, u32[]{:S(2)}, u32[]{:S(2)}) collective-permute-start(f32[1,4,64,128]{3,2,1,0:T(8,128)S(1)} %get-tuple-element.43.refs_0_), channel_id=1, source_target_pairs={{0,64},{64,128},{128,192},{192,0},{1,65},{65,129},{129,193},{193,1... | collective-permute-start | bytes 393224 | tf_op jit(solution)/shard_map/ppermute | solution.py:356
where the time goes:
time: 56.1 us; the launch traced here: 55.3 us
  starting transfers between devices  24.7 us (44%)
  Pallas kernels  19 us (34%)
  waiting for transfers between devices  11.5 us (20%)
    ppermute x7, starting transfers between devices, on_device(): down = lambda x: lax.ppermute(x, 'row', ring(-1))  15.2 us
    ppermute x7, waiting for transfers between devices, on_device(): up = lambda x: lax.ppermute(x, 'row', ring(1))  9.58 us
    pallas_call x3, Pallas kernels, right_products(): pl.pallas_call(functools.partial(right_kernel, which, sizes, len(after)),...  9.34 us
    pallas_call x1, Pallas kernels, left_products(): pl.pallas_call(functools.partial(left_kernel, lax.axis_size('slab')), out...  8.54 us
    ppermute x7, starting transfers between devices, on_device(): up = lambda x: lax.ppermute(x, 'row', ring(1))  4.26 us
    ppermute x1, starting transfers between devices, on_device(): from_far = lax.ppermute(p_tiles, 'row', ring(2))  3.02 us
    ppermute x1, starting transfers between devices, on_device(): from_other = lax.ppermute(stacked, 'slab', others)  2.11 us
    ppermute x7, waiting for transfers between devices, on_device(): down = lambda x: lax.ppermute(x, 'row', ring(-1))  1.89 us
  transfers between devices with their start and end apart: 17, of which 5 were waited for; matrix products, arithmetic and copies ran while one was open for 0% of the time, Pallas kernels for 33%

commit v1 on v0

--- a/solution.py
+++ b/solution.py
@@ -380,7 +380,7 @@
     twin_sums = add_shares(twin[3], twin_up, twin[4], twin_down, (other[0],))
     twin_two = up(twin_sums[0]), down(twin_sums[1])
     other_sums = add_shares(
-        other[3], other_up, other[4], other_down, (twin_sums[0],)
+        other[3], other_up, other[4], other_down, (twin_two[0],)
     )
     other_two = up(other_sums[0]), down(other_sums[1])
     out = finish(

time: 56.1 us -> 53.9 us (0.961)
  the two profiles are of different devices: /device:TPU:136 before, /device:TPU:86 now
where the time goes in v1:
time: 53.9 us; the launch traced here: 53.7 us
  starting transfers between devices  18.6 us (35%)
  Pallas kernels  18.3 us (34%)
  waiting for transfers between devices  16.8 us (31%)
    ppermute x7, starting transfers between devices, on_device(): up = lambda x: lax.ppermute(x, 'row', ring(1))  10.4 us
    ppermute x7, waiting for transfers between devices, on_device(): down = lambda x: lax.ppermute(x, 'row', ring(-1))  9.8 us
    pallas_call x3, Pallas kernels, right_products(): pl.pallas_call(functools.partial(right_kernel, which, sizes, len(after)),...  8.57 us
    pallas_call x1, Pallas kernels, left_products(): pl.pallas_call(functools.partial(left_kernel, lax.axis_size('slab')), out...  8.54 us
    ppermute x7, waiting for transfers between devices, on_device(): up = lambda x: lax.ppermute(x, 'row', ring(1))  6.96 us
    ppermute x7, starting transfers between devices, on_device(): down = lambda x: lax.ppermute(x, 'row', ring(-1))  4.56 us
    ppermute x1, starting transfers between devices, on_device(): from_other = lax.ppermute(stacked, 'slab', others)  2.1 us
    ppermute x1, starting transfers between devices, on_device(): from_far = lax.ppermute(p_tiles, 'row', ring(2))  1.41 us
  transfers between devices with their start and end apart: 17, of which 10 were waited for; matrix products, arithmetic and copies ran while one was open for 0% of the time, Pallas kernels for 32%

profile of v1, /device:TPU:86, one launch (start us, length us, event | category | flops | bytes accessed | tf_op | source)
XLA Modules:
  0.0 53.7 jit_solution(17267976155518642048)
XLA Ops:
  0.0 1.4 %collective-permute-start.1 = (f32[8,4096]{1,0:T(8,128)}, f32[8,4096]{1,0:T(8,128)S(1)}, u32[]{:S(2)}, u32[]{:S(2)}) collective-permute-start(f32[8,4096]{1,0:T(8,128)} %refs_0_.1), channel_id=1, source_target_pairs={{0,128},{64,192},{128,0},{192,64},{1,129},{65,193},{129,1},{193,65... | collective-permute-start | bytes 393224 | tf_op jit(solution)/shard_map/ppermute | solution.py:359
  1.4 0.0 collective-permute-start
  1.4 3.2 %collective-permute-start.2 = (f32[8,4096]{1,0:T(8,128)}, f32[8,4096]{1,0:T(8,128)S(1)}, u32[]{:S(2)}, u32[]{:S(2)}) collective-permute-start(f32[8,4096]{1,0:T(8,128)} %refs_0_.1), channel_id=1, source_target_pairs={{0,64},{64,128},{128,192},{192,0},{1,65},{65,129},{129,193},{193,1... | collective-permute-start | bytes 393224 | tf_op jit(solution)/shard_map/ppermute | solution.py:356
  4.6 8.5 %left_products.1 = (bf16[216,64,128]{2,1,0:T(8,128)(2,1)S(1)}, s32[675]{0:T(1024)S(1)}) custom-call(f32[6912,128]{1,0:T(8,128)} %bitcast.8, f32[8,4096]{1,0:T(8,128)} %refs_0_.1, s32[8,27]{1,0:T(8,128)} %cols_hbm.1, s32[8]{0:T(128)} %counts_hbm.1, s32[4,1,128]{2,1,0:T(1,128)} %refs_1_.5, s32[1,1,8]{2,1,0:T(1,128)} %owners_hbm.1), custom_call_target="tpu_custom_call" | custom-call | flops 4000000000 | bytes 8000000 | tf_op jit(solution)/shard_map/left_products/pallas_call | solution.py:159
  13.2 0.0 collective-permute-done.refs_1_
  13.3 0.1 collective-permute-start.5
  13.4 2.1 %collective-permute-start.10 = (f32[32,4096]{1,0:T(8,128)S(1)}, f32[32,4096]{1,0:T(8,128)S(1)}, u32[]{:S(2)}, u32[]{:S(2)}) collective-permute-start(f32[32,4096]{1,0:T(8,128)S(1)} %stack.1.refs_3_), channel_id=1, source_target_pairs={{1,2},{2,1},{3,4},{4,3},{5,6},{6,5},{7,8},{8,7},{9,10},{10,9},{11,... | collective-permute-start | bytes 1572872 | tf_op jit(solution)/shard_map/ppermute | solution.py:367
  15.5 3.0 %right_products.3 = (f32[2,4,64,128]{3,2,1,0:T(8,128)S(1)}, f32[2,4,64,128]{3,2,1,0:T(8,128)S(1)}, f32[2,4,64,128]{3,2,1,0:T(8,128)S(1)}, f32[1,4,64,128]{3,2,1,0:T(8,128)S(1)}, f32[1,4,64,128]{3,2,1,0:T(8,128)S(1)}) custom-call(s32[675]{0:T(1024)S(1)} %get-tuple-element.28.refs_4_.refs_0_, s32[4,1,128]{2,1,0:T(1,128)S(1)} %copy-done.1, ...), custom_call_target="tpu_custom_call" | custom-call | flops 3000000000 | bytes 5000000 | tf_op jit(solution)/shard_map/right_products/pallas_call | solution.py:261
  18.5 1.2 %collective-permute-start.3 = (f32[2,4,64,128]{3,2,1,0:T(8,128)S(1)}, f32[2,4,64,128]{3,2,1,0:T(8,128)S(1)}, u32[]{:S(2)}, u32[]{:S(2)}) collective-permute-start(f32[2,4,64,128]{3,2,1,0:T(8,128)S(1)} %get-tuple-element.31), channel_id=1, source_target_pairs={{0,64},{64,128},{128,192},{192,0},{1,65},{65,129},{129,193},{193,1... | collective-permute-start | bytes 786440 | tf_op jit(solution)/shard_map/ppermute | solution.py:356
  19.7 0.9 %collective-permute-start.4 = (f32[2,4,64,128]{3,2,1,0:T(8,128)S(1)}, f32[2,4,64,128]{3,2,1,0:T(8,128)S(1)}, u32[]{:S(2)}, u32[]{:S(2)}) collective-permute-start(f32[2,4,64,128]{3,2,1,0:T(8,128)S(1)} %get-tuple-element.32), channel_id=1, source_target_pairs={{0,192},{64,0},{128,64},{192,128},{1,193},{65,1},{129,65},{193,129... | collective-permute-start | bytes 786440 | tf_op jit(solution)/shard_map/ppermute | solution.py:357
  20.6 2.8 %right_products.4 = (f32[2,4,64,128]{3,2,1,0:T(8,128)S(1)}, f32[2,4,64,128]{3,2,1,0:T(8,128)S(1)}, f32[2,4,64,128]{3,2,1,0:T(8,128)S(1)}, f32[1,4,64,128]{3,2,1,0:T(8,128)S(1)}, f32[1,4,64,128]{3,2,1,0:T(8,128)S(1)}) custom-call(s32[675]{0:T(1024)S(1)} %get-tuple-element.28.refs_4_.refs_0_, s32[4,1,128]{2,1,0:T(1,128)S(1)} %copy-done.1, ...), custom_call_target="tpu_custom_call" | custom-call | flops 3000000000 | bytes 5000000 | tf_op jit(solution)/shard_map/right_products/pallas_call | solution.py:261
  23.4 2.7 %collective-permute-start.8 = (f32[2,4,64,128]{3,2,1,0:T(8,128)S(1)}, f32[2,4,64,128]{3,2,1,0:T(8,128)S(1)}, u32[]{:S(2)}, u32[]{:S(2)}) collective-permute-start(f32[2,4,64,128]{3,2,1,0:T(8,128)S(1)} %get-tuple-element.38), channel_id=1, source_target_pairs={{0,64},{64,128},{128,192},{192,0},{1,65},{65,129},{129,193},{193,1... | collective-permute-start | bytes 786440 | tf_op jit(solution)/shard_map/ppermute | solution.py:356
  26.1 1.4 %collective-permute-done.3.up_one.refs_1_ = f32[2,4,64,128]{3,2,1,0:T(8,128)S(1)} collective-permute-done((f32[2,4,64,128]{3,2,1,0:T(8,128)S(1)}, f32[2,4,64,128]{3,2,1,0:T(8,128)S(1)}, u32[]{:S(2)}, u32[]{:S(2)}) %collective-permute-start.3) | collective-permute-done | bytes 262176 | tf_op jit(solution)/shard_map/ppermute | solution.py:356
  27.5 2.1 %collective-permute-done.4.down_one.refs_2_ = f32[2,4,64,128]{3,2,1,0:T(8,128)S(1)} collective-permute-done((f32[2,4,64,128]{3,2,1,0:T(8,128)S(1)}, f32[2,4,64,128]{3,2,1,0:T(8,128)S(1)}, u32[]{:S(2)}, u32[]{:S(2)}) %collective-permute-start.4) | collective-permute-done | bytes 262176 | tf_op jit(solution)/shard_map/ppermute | solution.py:357
  29.6 2.8 %right_products.5 = (f32[2,4,64,128]{3,2,1,0:T(8,128)S(1)}, f32[2,4,64,128]{3,2,1,0:T(8,128)S(1)}, f32[2,4,64,128]{3,2,1,0:T(8,128)S(1)}, f32[1,4,64,128]{3,2,1,0:T(8,128)S(1)}, f32[1,4,64,128]{3,2,1,0:T(8,128)S(1)}) custom-call(s32[675]{0:T(1024)S(1)} %get-tuple-element.28.refs_4_.refs_0_, s32[4,1,128]{2,1,0:T(1,128)S(1)} %copy-done.1, ...), custom_call_target="tpu_custom_call" | custom-call | flops 3000000000 | bytes 5000000 | tf_op jit(solution)/shard_map/right_products/pallas_call | solution.py:261
  32.4 0.8 %collective-permute-start.13 = (f32[2,4,64,128]{3,2,1,0:T(8,128)S(1)}, f32[2,4,64,128]{3,2,1,0:T(8,128)S(1)}, u32[]{:S(2)}, u32[]{:S(2)}) collective-permute-start(f32[2,4,64,128]{3,2,1,0:T(8,128)S(1)} %get-tuple-element.45), channel_id=1, source_target_pairs={{0,64},{64,128},{128,192},{192,0},{1,65},{65,129},{129,193},{193,1... | collective-permute-start | bytes 786440 | tf_op jit(solution)/shard_map/ppermute | solution.py:356
  33.3 1.3 %collective-permute-start.14 = (f32[2,4,64,128]{3,2,1,0:T(8,128)S(1)}, f32[2,4,64,128]{3,2,1,0:T(8,128)S(1)}, u32[]{:S(2)}, u32[]{:S(2)}) collective-permute-start(f32[2,4,64,128]{3,2,1,0:T(8,128)S(1)} %get-tuple-element.46), channel_id=1, source_target_pairs={{0,192},{64,0},{128,64},{192,128},{1,193},{65,1},{129,65},{193,129... | collective-permute-start | bytes 786440 | tf_op jit(solution)/shard_map/ppermute | solution.py:357
  34.5 1.9 %collective-permute-done.9.down_one.refs_7_ = f32[2,4,64,128]{3,2,1,0:T(8,128)S(1)} collective-permute-done((f32[2,4,64,128]{3,2,1,0:T(8,128)S(1)}, f32[2,4,64,128]{3,2,1,0:T(8,128)S(1)}, u32[]{:S(2)}, u32[]{:S(2)}) %collective-permute-start.9) | collective-permute-done | bytes 262176 | tf_op jit(solution)/shard_map/ppermute | solution.py:357
  36.5 0.3 collective-permute-start.11
  36.8 0.1 collective-permute-start.6
  36.9 2.0 %collective-permute-start.7 = (f32[1,4,64,128]{3,2,1,0:T(8,128)S(1)}, f32[1,4,64,128]{3,2,1,0:T(8,128)S(1)}, u32[]{:S(2)}, u32[]{:S(2)}) collective-permute-start(f32[1,4,64,128]{3,2,1,0:T(8,128)S(1)} %get-tuple-element.37), channel_id=1, source_target_pairs={{0,192},{64,0},{128,64},{192,128},{1,193},{65,1},{129,65},{193,129... | collective-permute-start | bytes 393224 | tf_op jit(solution)/shard_map/ppermute | solution.py:357
  38.9 2.7 %collective-permute-done.13.up_one.refs_11_ = f32[2,4,64,128]{3,2,1,0:T(8,128)S(1)} collective-permute-done((f32[2,4,64,128]{3,2,1,0:T(8,128)S(1)}, f32[2,4,64,128]{3,2,1,0:T(8,128)S(1)}, u32[]{:S(2)}, u32[]{:S(2)}) %collective-permute-start.13) | collective-permute-done | bytes 262176 | tf_op jit(solution)/shard_map/ppermute | solution.py:356
  41.6 0.4 collective-permute-start.12
  42.0 1.7 %collective-permute-done.14.down_one.refs_12_ = f32[2,4,64,128]{3,2,1,0:T(8,128)S(1)} collective-permute-done((f32[2,4,64,128]{3,2,1,0:T(8,128)S(1)}, f32[2,4,64,128]{3,2,1,0:T(8,128)S(1)}, u32[]{:S(2)}, u32[]{:S(2)}) %collective-permute-start.14) | collective-permute-done | bytes 262176 | tf_op jit(solution)/shard_map/ppermute | solution.py:357
  43.7 0.8 %collective-permute-done.11.refs_0_.refs_8_ = f32[1,4,64,128]{3,2,1,0:T(8,128)S(1)} collective-permute-done((f32[1,4,64,128]{3,2,1,0:T(8,128)S(1)}, f32[1,4,64,128]{3,2,1,0:T(8,128)S(1)}, u32[]{:S(2)}, u32[]{:S(2)}) %collective-permute-start.11) | collective-permute-done | bytes 131104 | tf_op jit(solution)/shard_map/ppermute | solution.py:356
  44.5 2.1 %collective-permute-start.15 = (f32[1,4,64,128]{3,2,1,0:T(8,128)S(1)}, f32[1,4,64,128]{3,2,1,0:T(8,128)S(1)}, u32[]{:S(2)}, u32[]{:S(2)}) collective-permute-start(f32[1,4,64,128]{3,2,1,0:T(8,128)S(1)} %get-tuple-element.49), channel_id=1, source_target_pairs={{0,64},{64,128},{128,192},{192,0},{1,65},{65,129},{129,193},{193,1... | collective-permute-start | bytes 393224 | tf_op jit(solution)/shard_map/ppermute | solution.py:356
  46.6 0.0 collective-permute-start.16
  46.6 0.6 %collective-permute-done.6.refs_3_ = f32[1,4,64,128]{3,2,1,0:T(8,128)S(1)} collective-permute-done((f32[1,4,64,128]{3,2,1,0:T(8,128)S(1)}, f32[1,4,64,128]{3,2,1,0:T(8,128)S(1)}, u32[]{:S(2)}, u32[]{:S(2)}) %collective-permute-start.6) | collective-permute-done | bytes 131104 | tf_op jit(solution)/shard_map/ppermute | solution.py:356
  47.2 1.1 %collective-permute-done.12.refs_9_ = f32[1,4,64,128]{3,2,1,0:T(8,128)S(1)} collective-permute-done((f32[1,4,64,128]{3,2,1,0:T(8,128)S(1)}, f32[1,4,64,128]{3,2,1,0:T(8,128)S(1)}, u32[]{:S(2)}, u32[]{:S(2)}) %collective-permute-start.12) | collective-permute-done | bytes 131104 | tf_op jit(solution)/shard_map/ppermute | solution.py:357
  48.2 1.5 %collective-permute-done.15.refs_13_ = f32[1,4,64,128]{3,2,1,0:T(8,128)S(1)} collective-permute-done((f32[1,4,64,128]{3,2,1,0:T(8,128)S(1)}, f32[1,4,64,128]{3,2,1,0:T(8,128)S(1)}, u32[]{:S(2)}, u32[]{:S(2)}) %collective-permute-start.15) | collective-permute-done | bytes 131104 | tf_op jit(solution)/shard_map/ppermute | solution.py:356
  49.8 3.0 %collective-permute-done.16.refs_14_ = f32[1,4,64,128]{3,2,1,0:T(8,128)S(1)} collective-permute-done((f32[1,4,64,128]{3,2,1,0:T(8,128)S(1)}, f32[1,4,64,128]{3,2,1,0:T(8,128)S(1)}, u32[]{:S(2)}, u32[]{:S(2)}) %collective-permute-start.16) | collective-permute-done | bytes 131104 | tf_op jit(solution)/shard_map/ppermute | solution.py:357
  52.7 1.0 %finish.1 = f32[2,64,1536]{2,1,0:T(8,128)} custom-call(f32[2,4,64,128]{3,2,1,0:T(8,128)S(1)} %get-tuple-element.30.refs_4_.refs_0_, f32[2,4,64,128]{3,2,1,0:T(8,128)S(1)} %collective-permute-done.3.up_one.refs_1_, f32[2,4,64,128]{3,2,1,0:T(8,128)S(1)} %collective-permute-done.4.down_one.refs_2_, f32[1,4,64,128]{3,2,1,0:T(8,128)S(1)} %collective-permute-done.6.refs_3_, ...), custom_call_target="tpu_custom_call" | custom-call | tf_op jit(solution)/shard_map/finish/pallas_call | solution.py:319
  (15 shorter events, 0.2 us)
Async XLA Ops:
  0.0 13.2 %collective-permute-start.1 = (f32[8,4096]{1,0:T(8,128)}, f32[8,4096]{1,0:T(8,128)S(1)}, u32[]{:S(2)}, u32[]{:S(2)}) collective-permute-start(f32[8,4096]{1,0:T(8,128)} %refs_0_.1), channel_id=1, source_target_pairs={{0,128},{64,192},{128,0},{192,64},{1,129},{65,193},{129,1},{193,65... | collective-permute-start | bytes 393224 | tf_op jit(solution)/shard_map/ppermute | solution.py:359
  1.4 11.8 %collective-permute-start = (f32[8,4096]{1,0:T(8,128)}, f32[8,4096]{1,0:T(8,128)S(1)}, u32[]{:S(2)}, u32[]{:S(2)}) collective-permute-start(f32[8,4096]{1,0:T(8,128)} %refs_0_.1), channel_id=1, source_target_pairs={{0,192},{64,0},{128,64},{192,128},{1,193},{65,1},{129,65},{193,129... | collective-permute-start | bytes 393224 | tf_op jit(solution)/shard_map/ppermute | solution.py:357
  1.4 11.8 %collective-permute-start.2 = (f32[8,4096]{1,0:T(8,128)}, f32[8,4096]{1,0:T(8,128)S(1)}, u32[]{:S(2)}, u32[]{:S(2)}) collective-permute-start(f32[8,4096]{1,0:T(8,128)} %refs_0_.1), channel_id=1, source_target_pairs={{0,64},{64,128},{128,192},{192,0},{1,65},{65,129},{129,193},{193,1... | collective-permute-start | bytes 393224 | tf_op jit(solution)/shard_map/ppermute | solution.py:356
  4.6 8.6 %copy-start = (f32[8,4096]{1,0:T(8,128)S(1)}, f32[8,4096]{1,0:T(8,128)}, u32[]{:S(2)}) copy-start(f32[8,4096]{1,0:T(8,128)} %refs_0_.1) | copy-start | bytes 393220
  4.6 10.8 %copy-start.1 = (s32[4,1,128]{2,1,0:T(1,128)S(1)}, s32[4,1,128]{2,1,0:T(1,128)}, u32[]{:S(2)}) copy-start(s32[4,1,128]{2,1,0:T(1,128)} %refs_1_.5) | copy-start | bytes 6148
  13.3 7.4 %collective-permute-start.5 = (f32[32,4096]{1,0:T(8,128)S(1)}, f32[32,4096]{1,0:T(8,128)S(1)}, u32[]{:S(2)}, u32[]{:S(2)}) collective-permute-start(f32[32,4096]{1,0:T(8,128)S(1)} %stack.1.refs_3_), channel_id=1, source_target_pairs={{0,1},{1,0},{2,3},{3,2},{4,5},{5,4},{6,7},{7,6},{8,9},{9,8},{10,11... | collective-permute-start | bytes 1572872 | tf_op jit(solution)/shard_map/ppermute | solution.py:368
  13.4 16.3 %collective-permute-start.10 = (f32[32,4096]{1,0:T(8,128)S(1)}, f32[32,4096]{1,0:T(8,128)S(1)}, u32[]{:S(2)}, u32[]{:S(2)}) collective-permute-start(f32[32,4096]{1,0:T(8,128)S(1)} %stack.1.refs_3_), channel_id=1, source_target_pairs={{1,2},{2,1},{3,4},{4,3},{5,6},{6,5},{7,8},{8,7},{9,10},{10,9},{11,... | collective-permute-start | bytes 1572872 | tf_op jit(solution)/shard_map/ppermute | solution.py:367
  18.5 8.9 %collective-permute-start.3 = (f32[2,4,64,128]{3,2,1,0:T(8,128)S(1)}, f32[2,4,64,128]{3,2,1,0:T(8,128)S(1)}, u32[]{:S(2)}, u32[]{:S(2)}) collective-permute-start(f32[2,4,64,128]{3,2,1,0:T(8,128)S(1)} %get-tuple-element.31), channel_id=1, source_target_pairs={{0,64},{64,128},{128,192},{192,0},{1,65},{65,129},{129,193},{193,1... | collective-permute-start | bytes 786440 | tf_op jit(solution)/shard_map/ppermute | solution.py:356
  19.7 9.9 %collective-permute-start.4 = (f32[2,4,64,128]{3,2,1,0:T(8,128)S(1)}, f32[2,4,64,128]{3,2,1,0:T(8,128)S(1)}, u32[]{:S(2)}, u32[]{:S(2)}) collective-permute-start(f32[2,4,64,128]{3,2,1,0:T(8,128)S(1)} %get-tuple-element.32), channel_id=1, source_target_pairs={{0,192},{64,0},{128,64},{192,128},{1,193},{65,1},{129,65},{193,129... | collective-permute-start | bytes 786440 | tf_op jit(solution)/shard_map/ppermute | solution.py:357
  23.4 11.1 %collective-permute-start.8 = (f32[2,4,64,128]{3,2,1,0:T(8,128)S(1)}, f32[2,4,64,128]{3,2,1,0:T(8,128)S(1)}, u32[]{:S(2)}, u32[]{:S(2)}) collective-permute-start(f32[2,4,64,128]{3,2,1,0:T(8,128)S(1)} %get-tuple-element.38), channel_id=1, source_target_pairs={{0,64},{64,128},{128,192},{192,0},{1,65},{65,129},{129,193},{193,1... | collective-permute-start | bytes 786440 | tf_op jit(solution)/shard_map/ppermute | solution.py:356
  26.1 10.4 %collective-permute-start.9 = (f32[2,4,64,128]{3,2,1,0:T(8,128)S(1)}, f32[2,4,64,128]{3,2,1,0:T(8,128)S(1)}, u32[]{:S(2)}, u32[]{:S(2)}) collective-permute-start(f32[2,4,64,128]{3,2,1,0:T(8,128)S(1)} %get-tuple-element.39), channel_id=1, source_target_pairs={{0,192},{64,0},{128,64},{192,128},{1,193},{65,1},{129,65},{193,129... | collective-permute-start | bytes 786440 | tf_op jit(solution)/shard_map/ppermute | solution.py:357
  32.4 9.2 %collective-permute-start.13 = (f32[2,4,64,128]{3,2,1,0:T(8,128)S(1)}, f32[2,4,64,128]{3,2,1,0:T(8,128)S(1)}, u32[]{:S(2)}, u32[]{:S(2)}) collective-permute-start(f32[2,4,64,128]{3,2,1,0:T(8,128)S(1)} %get-tuple-element.45), channel_id=1, source_target_pairs={{0,64},{64,128},{128,192},{192,0},{1,65},{65,129},{129,193},{193,1... | collective-permute-start | bytes 786440 | tf_op jit(solution)/shard_map/ppermute | solution.py:356
  33.3 10.4 %collective-permute-start.14 = (f32[2,4,64,128]{3,2,1,0:T(8,128)S(1)}, f32[2,4,64,128]{3,2,1,0:T(8,128)S(1)}, u32[]{:S(2)}, u32[]{:S(2)}) collective-permute-start(f32[2,4,64,128]{3,2,1,0:T(8,128)S(1)} %get-tuple-element.46), channel_id=1, source_target_pairs={{0,192},{64,0},{128,64},{192,128},{1,193},{65,1},{129,65},{193,129... | collective-permute-start | bytes 786440 | tf_op jit(solution)/shard_map/ppermute | solution.py:357
  36.5 7.9 %collective-permute-start.11 = (f32[1,4,64,128]{3,2,1,0:T(8,128)S(1)}, f32[1,4,64,128]{3,2,1,0:T(8,128)S(1)}, u32[]{:S(2)}, u32[]{:S(2)}) collective-permute-start(f32[1,4,64,128]{3,2,1,0:T(8,128)S(1)} %get-tuple-element.43), channel_id=1, source_target_pairs={{0,64},{64,128},{128,192},{192,0},{1,65},{65,129},{129,193},{193,1... | collective-permute-start | bytes 393224 | tf_op jit(solution)/shard_map/ppermute | solution.py:356
  36.8 10.3 %collective-permute-start.6 = (f32[1,4,64,128]{3,2,1,0:T(8,128)S(1)}, f32[1,4,64,128]{3,2,1,0:T(8,128)S(1)}, u32[]{:S(2)}, u32[]{:S(2)}) collective-permute-start(f32[1,4,64,128]{3,2,1,0:T(8,128)S(1)} %get-tuple-element.36.refs_5_), channel_id=1, source_target_pairs={{0,64},{64,128},{128,192},{192,0},{1,65},{65,129},{129,193},{193,1... | collective-permute-start | bytes 393224 | tf_op jit(solution)/shard_map/ppermute | solution.py:356
  36.9 9.7 %collective-permute-start.7 = (f32[1,4,64,128]{3,2,1,0:T(8,128)S(1)}, f32[1,4,64,128]{3,2,1,0:T(8,128)S(1)}, u32[]{:S(2)}, u32[]{:S(2)}) collective-permute-start(f32[1,4,64,128]{3,2,1,0:T(8,128)S(1)} %get-tuple-element.37), channel_id=1, source_target_pairs={{0,192},{64,0},{128,64},{192,128},{1,193},{65,1},{129,65},{193,129... | collective-permute-start | bytes 393224 | tf_op jit(solution)/shard_map/ppermute | solution.py:357
  41.6 6.6 %collective-permute-start.12 = (f32[1,4,64,128]{3,2,1,0:T(8,128)S(1)}, f32[1,4,64,128]{3,2,1,0:T(8,128)S(1)}, u32[]{:S(2)}, u32[]{:S(2)}) collective-permute-start(f32[1,4,64,128]{3,2,1,0:T(8,128)S(1)} %get-tuple-element.44), channel_id=1, source_target_pairs={{0,192},{64,0},{128,64},{192,128},{1,193},{65,1},{129,65},{193,129... | collective-permute-start | bytes 393224 | tf_op jit(solution)/shard_map/ppermute | solution.py:357
  44.5 5.3 %collective-permute-start.15 = (f32[1,4,64,128]{3,2,1,0:T(8,128)S(1)}, f32[1,4,64,128]{3,2,1,0:T(8,128)S(1)}, u32[]{:S(2)}, u32[]{:S(2)}) collective-permute-start(f32[1,4,64,128]{3,2,1,0:T(8,128)S(1)} %get-tuple-element.49), channel_id=1, source_target_pairs={{0,64},{64,128},{128,192},{192,0},{1,65},{65,129},{129,193},{193,1... | collective-permute-start | bytes 393224 | tf_op jit(solution)/shard_map/ppermute | solution.py:356
  46.6 6.2 %collective-permute-start.16 = (f32[1,4,64,128]{3,2,1,0:T(8,128)S(1)}, f32[1,4,64,128]{3,2,1,0:T(8,128)S(1)}, u32[]{:S(2)}, u32[]{:S(2)}) collective-permute-start(f32[1,4,64,128]{3,2,1,0:T(8,128)S(1)} %get-tuple-element.50), channel_id=1, source_target_pairs={{0,192},{64,0},{128,64},{192,128},{1,193},{65,1},{129,65},{193,129... | collective-permute-start | bytes 393224 | tf_op jit(solution)/shard_map/ppermute | solution.py:357

commit v2 on v1

--- a/solution.py
+++ b/solution.py
@@ -110,14 +110,6 @@
                         k < counts[i],
                     )
                 )
-        for entry, is_own, is_pair, live in entries:
-            todo[jnp.where(is_own, own_at, jnp.where(is_pair, pair_at, far_at))] = entry
-            one = live.astype(jnp.int32)
-            own_one = jnp.where(is_own, one, 0)
-            pair_one = jnp.where(is_pair, one, 0)
-            own_at = own_at + own_one
-            pair_at = pair_at + pair_one
-            far_at = far_at + (one - own_one - pair_one)
         for i in range(RB):
             lhs = lhs_buf[i]
             parts = []
@@ -140,6 +132,14 @@
                 t_ref[(n * GROUP + u) * RB + i] = jnp.where(
                     first_out, one, rest
                 ).astype(bf16)
+        for entry, is_own, is_pair, live in entries:
+            todo[jnp.where(is_own, own_at, jnp.where(is_pair, pair_at, far_at))] = entry
+            one = live.astype(jnp.int32)
+            own_one = jnp.where(is_own, one, 0)
+            pair_one = jnp.where(is_pair, one, 0)
+            own_at = own_at + own_one
+            pair_at = pair_at + pair_one
+            far_at = far_at + (one - own_one - pair_one)
         return own_at, pair_at, far_at
 
     starts = tuple(jnp.int32(g * LIST) for g in range(3))

time: 53.9 us -> 54.1 us (level); the launches traced: 53.7 us -> 53.1 us
  waiting for transfers between devices: 16.8 us -> 16.2 us
    ppermute x7, waiting for transfers between devices: 9.8 us -> 7.2 us  [on_device(): down = lambda x: lax.ppermute(x, 'row', ring(-1))]
    ppermute x7, starting transfers between devices: 10.4 us -> 7.84 us  [on_device(): up = lambda x: lax.ppermute(x, 'row', ring(1))]
    ppermute x7, starting transfers between devices: 4.56 us -> 6.82 us  [on_device(): down = lambda x: lax.ppermute(x, 'row', ring(-1))]
    ppermute x7, waiting for transfers between devices: 6.96 us -> 8.97 us  [on_device(): up = lambda x: lax.ppermute(x, 'row', ring(1))]
  transfers between devices with their start and end apart: 17 -> 17, of which waited for: 10 -> 10; matrix products, arithmetic and copies ran while one was open for 0% -> 0% of each run, Pallas kernels for 32% -> 33%
where the time goes in v2:
time: 54.1 us; the launch traced here: 53.1 us
  Pallas kernels  18.6 us (34%)
  starting transfers between devices  18.3 us (34%)
  waiting for transfers between devices  16.2 us (30%)
    ppermute x7, waiting for transfers between devices, on_device(): up = lambda x: lax.ppermute(x, 'row', ring(1))  8.97 us
    pallas_call x3, Pallas kernels, right_products(): pl.pallas_call(functools.partial(right_kernel, which, sizes, len(after)),...  8.87 us
    pallas_call x1, Pallas kernels, left_products(): pl.pallas_call(functools.partial(left_kernel, lax.axis_size('slab')), out...  8.54 us
    ppermute x7, starting transfers between devices, on_device(): up = lambda x: lax.ppermute(x, 'row', ring(1))  7.84 us
    ppermute x7, waiting for transfers between devices, on_device(): down = lambda x: lax.ppermute(x, 'row', ring(-1))  7.2 us
    ppermute x7, starting transfers between devices, on_device(): down = lambda x: lax.ppermute(x, 'row', ring(-1))  6.82 us
    ppermute x1, starting transfers between devices, on_device(): from_other = lax.ppermute(stacked, 'slab', others)  2.1 us
    ppermute x1, starting transfers between devices, on_device(): from_far = lax.ppermute(p_tiles, 'row', ring(2))  1.41 us
  transfers between devices with their start and end apart: 17, of which 10 were waited for; matrix products, arithmetic and copies ran while one was open for 0% of the time, Pallas kernels for 33%

profile of v2, /device:TPU:86, one launch (start us, length us, event | category | flops | bytes accessed | tf_op | source)
XLA Modules:
  0.0 53.1 jit_solution(17267976155518642048)
XLA Ops:
  0.0 1.4 %collective-permute-start.1 = (f32[8,4096]{1,0:T(8,128)}, f32[8,4096]{1,0:T(8,128)S(1)}, u32[]{:S(2)}, u32[]{:S(2)}) collective-permute-start(f32[8,4096]{1,0:T(8,128)} %refs_0_.1), channel_id=1, source_target_pairs={{0,128},{64,192},{128,0},{192,64},{1,129},{65,193},{129,1},{193,65... | collective-permute-start | bytes 393224 | tf_op jit(solution)/shard_map/ppermute | solution.py:359
  1.4 3.2 %collective-permute-start.2 = (f32[8,4096]{1,0:T(8,128)}, f32[8,4096]{1,0:T(8,128)S(1)}, u32[]{:S(2)}, u32[]{:S(2)}) collective-permute-start(f32[8,4096]{1,0:T(8,128)} %refs_0_.1), channel_id=1, source_target_pairs={{0,64},{64,128},{128,192},{192,0},{1,65},{65,129},{129,193},{193,1... | collective-permute-start | bytes 393224 | tf_op jit(solution)/shard_map/ppermute | solution.py:356
  4.6 8.5 %left_products.1 = (bf16[216,64,128]{2,1,0:T(8,128)(2,1)S(1)}, s32[675]{0:T(1024)S(1)}) custom-call(f32[6912,128]{1,0:T(8,128)} %bitcast.8, f32[8,4096]{1,0:T(8,128)} %refs_0_.1, s32[8,27]{1,0:T(8,128)} %cols_hbm.1, s32[8]{0:T(128)} %counts_hbm.1, s32[4,1,128]{2,1,0:T(1,128)} %refs_1_.5, s32[1,1,8]{2,1,0:T(1,128)} %owners_hbm.1), custom_call_target="tpu_custom_call" | custom-call | flops 4000000000 | bytes 8000000 | tf_op jit(solution)/shard_map/left_products/pallas_call | solution.py:159
  13.2 0.0 collective-permute-done.1.refs_2_
  13.3 0.1 collective-permute-start.5
  13.4 2.1 %collective-permute-start.10 = (f32[32,4096]{1,0:T(8,128)S(1)}, f32[32,4096]{1,0:T(8,128)S(1)}, u32[]{:S(2)}, u32[]{:S(2)}) collective-permute-start(f32[32,4096]{1,0:T(8,128)S(1)} %stack.1.refs_3_), channel_id=1, source_target_pairs={{1,2},{2,1},{3,4},{4,3},{5,6},{6,5},{7,8},{8,7},{9,10},{10,9},{11,... | collective-permute-start | bytes 1572872 | tf_op jit(solution)/shard_map/ppermute | solution.py:367
  15.5 3.2 %right_products.3 = (f32[2,4,64,128]{3,2,1,0:T(8,128)S(1)}, f32[2,4,64,128]{3,2,1,0:T(8,128)S(1)}, f32[2,4,64,128]{3,2,1,0:T(8,128)S(1)}, f32[1,4,64,128]{3,2,1,0:T(8,128)S(1)}, f32[1,4,64,128]{3,2,1,0:T(8,128)S(1)}) custom-call(s32[675]{0:T(1024)S(1)} %get-tuple-element.28.refs_4_.refs_0_, s32[4,1,128]{2,1,0:T(1,128)S(1)} %copy-done.1, ...), custom_call_target="tpu_custom_call" | custom-call | flops 3000000000 | bytes 5000000 | tf_op jit(solution)/shard_map/right_products/pallas_call | solution.py:261
  18.8 0.7 %collective-permute-start.3 = (f32[2,4,64,128]{3,2,1,0:T(8,128)S(1)}, f32[2,4,64,128]{3,2,1,0:T(8,128)S(1)}, u32[]{:S(2)}, u32[]{:S(2)}) collective-permute-start(f32[2,4,64,128]{3,2,1,0:T(8,128)S(1)} %get-tuple-element.31), channel_id=1, source_target_pairs={{0,64},{64,128},{128,192},{192,0},{1,65},{65,129},{129,193},{193,1... | collective-permute-start | bytes 786440 | tf_op jit(solution)/shard_map/ppermute | solution.py:356
  19.5 1.4 %collective-permute-start.4 = (f32[2,4,64,128]{3,2,1,0:T(8,128)S(1)}, f32[2,4,64,128]{3,2,1,0:T(8,128)S(1)}, u32[]{:S(2)}, u32[]{:S(2)}) collective-permute-start(f32[2,4,64,128]{3,2,1,0:T(8,128)S(1)} %get-tuple-element.32), channel_id=1, source_target_pairs={{0,192},{64,0},{128,64},{192,128},{1,193},{65,1},{129,65},{193,129... | collective-permute-start | bytes 786440 | tf_op jit(solution)/shard_map/ppermute | solution.py:357
  20.9 2.8 %right_products.4 = (f32[2,4,64,128]{3,2,1,0:T(8,128)S(1)}, f32[2,4,64,128]{3,2,1,0:T(8,128)S(1)}, f32[2,4,64,128]{3,2,1,0:T(8,128)S(1)}, f32[1,4,64,128]{3,2,1,0:T(8,128)S(1)}, f32[1,4,64,128]{3,2,1,0:T(8,128)S(1)}) custom-call(s32[675]{0:T(1024)S(1)} %get-tuple-element.28.refs_4_.refs_0_, s32[4,1,128]{2,1,0:T(1,128)S(1)} %copy-done.1, ...), custom_call_target="tpu_custom_call" | custom-call | flops 3000000000 | bytes 5000000 | tf_op jit(solution)/shard_map/right_products/pallas_call | solution.py:261
  23.7 1.7 %collective-permute-start.8 = (f32[2,4,64,128]{3,2,1,0:T(8,128)S(1)}, f32[2,4,64,128]{3,2,1,0:T(8,128)S(1)}, u32[]{:S(2)}, u32[]{:S(2)}) collective-permute-start(f32[2,4,64,128]{3,2,1,0:T(8,128)S(1)} %get-tuple-element.38), channel_id=1, source_target_pairs={{0,64},{64,128},{128,192},{192,0},{1,65},{65,129},{129,193},{193,1... | collective-permute-start | bytes 786440 | tf_op jit(solution)/shard_map/ppermute | solution.py:356
  25.4 0.4 collective-permute-start.9
  25.8 1.7 %collective-permute-done.3.up_one.refs_1_ = f32[2,4,64,128]{3,2,1,0:T(8,128)S(1)} collective-permute-done((f32[2,4,64,128]{3,2,1,0:T(8,128)S(1)}, f32[2,4,64,128]{3,2,1,0:T(8,128)S(1)}, u32[]{:S(2)}, u32[]{:S(2)}) %collective-permute-start.3) | collective-permute-done | bytes 262176 | tf_op jit(solution)/shard_map/ppermute | solution.py:356
  27.4 2.3 %collective-permute-done.4.down_one.refs_2_ = f32[2,4,64,128]{3,2,1,0:T(8,128)S(1)} collective-permute-done((f32[2,4,64,128]{3,2,1,0:T(8,128)S(1)}, f32[2,4,64,128]{3,2,1,0:T(8,128)S(1)}, u32[]{:S(2)}, u32[]{:S(2)}) %collective-permute-start.4) | collective-permute-done | bytes 262176 | tf_op jit(solution)/shard_map/ppermute | solution.py:357
  29.8 2.8 %right_products.5 = (f32[2,4,64,128]{3,2,1,0:T(8,128)S(1)}, f32[2,4,64,128]{3,2,1,0:T(8,128)S(1)}, f32[2,4,64,128]{3,2,1,0:T(8,128)S(1)}, f32[1,4,64,128]{3,2,1,0:T(8,128)S(1)}, f32[1,4,64,128]{3,2,1,0:T(8,128)S(1)}) custom-call(s32[675]{0:T(1024)S(1)} %get-tuple-element.28.refs_4_.refs_0_, s32[4,1,128]{2,1,0:T(1,128)S(1)} %copy-done.1, ...), custom_call_target="tpu_custom_call" | custom-call | flops 3000000000 | bytes 5000000 | tf_op jit(solution)/shard_map/right_products/pallas_call | solution.py:261
  32.6 0.1 collective-permute-start.13
  32.7 2.0 %collective-permute-start.14 = (f32[2,4,64,128]{3,2,1,0:T(8,128)S(1)}, f32[2,4,64,128]{3,2,1,0:T(8,128)S(1)}, u32[]{:S(2)}, u32[]{:S(2)}) collective-permute-start(f32[2,4,64,128]{3,2,1,0:T(8,128)S(1)} %get-tuple-element.46), channel_id=1, source_target_pairs={{0,192},{64,0},{128,64},{192,128},{1,193},{65,1},{129,65},{193,129... | collective-permute-start | bytes 786440 | tf_op jit(solution)/shard_map/ppermute | solution.py:357
  34.7 0.8 %collective-permute-done.9.down_one.refs_7_ = f32[2,4,64,128]{3,2,1,0:T(8,128)S(1)} collective-permute-done((f32[2,4,64,128]{3,2,1,0:T(8,128)S(1)}, f32[2,4,64,128]{3,2,1,0:T(8,128)S(1)}, u32[]{:S(2)}, u32[]{:S(2)}) %collective-permute-start.9) | collective-permute-done | bytes 262176 | tf_op jit(solution)/shard_map/ppermute | solution.py:357
  35.5 0.8 %collective-permute-start.11 = (f32[1,4,64,128]{3,2,1,0:T(8,128)S(1)}, f32[1,4,64,128]{3,2,1,0:T(8,128)S(1)}, u32[]{:S(2)}, u32[]{:S(2)}) collective-permute-start(f32[1,4,64,128]{3,2,1,0:T(8,128)S(1)} %get-tuple-element.43), channel_id=1, source_target_pairs={{0,64},{64,128},{128,192},{192,0},{1,65},{65,129},{129,193},{193,1... | collective-permute-start | bytes 393224 | tf_op jit(solution)/shard_map/ppermute | solution.py:356
  36.3 0.1 collective-permute-start.6
  36.4 1.9 %collective-permute-start.7 = (f32[1,4,64,128]{3,2,1,0:T(8,128)S(1)}, f32[1,4,64,128]{3,2,1,0:T(8,128)S(1)}, u32[]{:S(2)}, u32[]{:S(2)}) collective-permute-start(f32[1,4,64,128]{3,2,1,0:T(8,128)S(1)} %get-tuple-element.37), channel_id=1, source_target_pairs={{0,192},{64,0},{128,64},{192,128},{1,193},{65,1},{129,65},{193,129... | collective-permute-start | bytes 393224 | tf_op jit(solution)/shard_map/ppermute | solution.py:357
  38.3 3.5 %collective-permute-done.13.up_one.refs_11_ = f32[2,4,64,128]{3,2,1,0:T(8,128)S(1)} collective-permute-done((f32[2,4,64,128]{3,2,1,0:T(8,128)S(1)}, f32[2,4,64,128]{3,2,1,0:T(8,128)S(1)}, u32[]{:S(2)}, u32[]{:S(2)}) %collective-permute-start.13) | collective-permute-done | bytes 262176 | tf_op jit(solution)/shard_map/ppermute | solution.py:356
  41.8 0.2 collective-permute-start.12
  42.1 1.1 %collective-permute-done.14.down_one.refs_12_ = f32[2,4,64,128]{3,2,1,0:T(8,128)S(1)} collective-permute-done((f32[2,4,64,128]{3,2,1,0:T(8,128)S(1)}, f32[2,4,64,128]{3,2,1,0:T(8,128)S(1)}, u32[]{:S(2)}, u32[]{:S(2)}) %collective-permute-start.14) | collective-permute-done | bytes 262176 | tf_op jit(solution)/shard_map/ppermute | solution.py:357
  43.1 1.5 %collective-permute-done.11.refs_0_.refs_8_ = f32[1,4,64,128]{3,2,1,0:T(8,128)S(1)} collective-permute-done((f32[1,4,64,128]{3,2,1,0:T(8,128)S(1)}, f32[1,4,64,128]{3,2,1,0:T(8,128)S(1)}, u32[]{:S(2)}, u32[]{:S(2)}) %collective-permute-start.11) | collective-permute-done | bytes 131104 | tf_op jit(solution)/shard_map/ppermute | solution.py:356
  44.7 1.3 %collective-permute-start.15 = (f32[1,4,64,128]{3,2,1,0:T(8,128)S(1)}, f32[1,4,64,128]{3,2,1,0:T(8,128)S(1)}, u32[]{:S(2)}, u32[]{:S(2)}) collective-permute-start(f32[1,4,64,128]{3,2,1,0:T(8,128)S(1)} %get-tuple-element.49), channel_id=1, source_target_pairs={{0,64},{64,128},{128,192},{192,0},{1,65},{65,129},{129,193},{193,1... | collective-permute-start | bytes 393224 | tf_op jit(solution)/shard_map/ppermute | solution.py:356
  45.9 0.8 %collective-permute-start.16 = (f32[1,4,64,128]{3,2,1,0:T(8,128)S(1)}, f32[1,4,64,128]{3,2,1,0:T(8,128)S(1)}, u32[]{:S(2)}, u32[]{:S(2)}) collective-permute-start(f32[1,4,64,128]{3,2,1,0:T(8,128)S(1)} %get-tuple-element.50), channel_id=1, source_target_pairs={{0,192},{64,0},{128,64},{192,128},{1,193},{65,1},{129,65},{193,129... | collective-permute-start | bytes 393224 | tf_op jit(solution)/shard_map/ppermute | solution.py:357
  46.8 0.6 %collective-permute-done.6.refs_3_ = f32[1,4,64,128]{3,2,1,0:T(8,128)S(1)} collective-permute-done((f32[1,4,64,128]{3,2,1,0:T(8,128)S(1)}, f32[1,4,64,128]{3,2,1,0:T(8,128)S(1)}, u32[]{:S(2)}, u32[]{:S(2)}) %collective-permute-start.6) | collective-permute-done | bytes 131104 | tf_op jit(solution)/shard_map/ppermute | solution.py:356
  47.4 0.6 %collective-permute-done.12.refs_9_ = f32[1,4,64,128]{3,2,1,0:T(8,128)S(1)} collective-permute-done((f32[1,4,64,128]{3,2,1,0:T(8,128)S(1)}, f32[1,4,64,128]{3,2,1,0:T(8,128)S(1)}, u32[]{:S(2)}, u32[]{:S(2)}) %collective-permute-start.12) | collective-permute-done | bytes 131104 | tf_op jit(solution)/shard_map/ppermute | solution.py:357
  48.0 1.7 %collective-permute-done.15.refs_13_ = f32[1,4,64,128]{3,2,1,0:T(8,128)S(1)} collective-permute-done((f32[1,4,64,128]{3,2,1,0:T(8,128)S(1)}, f32[1,4,64,128]{3,2,1,0:T(8,128)S(1)}, u32[]{:S(2)}, u32[]{:S(2)}) %collective-permute-start.15) | collective-permute-done | bytes 131104 | tf_op jit(solution)/shard_map/ppermute | solution.py:356
  49.7 2.4 %collective-permute-done.16.refs_14_ = f32[1,4,64,128]{3,2,1,0:T(8,128)S(1)} collective-permute-done((f32[1,4,64,128]{3,2,1,0:T(8,128)S(1)}, f32[1,4,64,128]{3,2,1,0:T(8,128)S(1)}, u32[]{:S(2)}, u32[]{:S(2)}) %collective-permute-start.16) | collective-permute-done | bytes 131104 | tf_op jit(solution)/shard_map/ppermute | solution.py:357
  52.1 1.0 %finish.1 = f32[2,64,1536]{2,1,0:T(8,128)} custom-call(f32[2,4,64,128]{3,2,1,0:T(8,128)S(1)} %get-tuple-element.30.refs_4_.refs_0_, f32[2,4,64,128]{3,2,1,0:T(8,128)S(1)} %collective-permute-done.3.up_one.refs_1_, f32[2,4,64,128]{3,2,1,0:T(8,128)S(1)} %collective-permute-done.4.down_one.refs_2_, f32[1,4,64,128]{3,2,1,0:T(8,128)S(1)} %collective-permute-done.6.refs_3_, ...), custom_call_target="tpu_custom_call" | custom-call | tf_op jit(solution)/shard_map/finish/pallas_call | solution.py:319
  (15 shorter events, 0.2 us)
Async XLA Ops:
  0.0 13.2 %collective-permute-start.1 = (f32[8,4096]{1,0:T(8,128)}, f32[8,4096]{1,0:T(8,128)S(1)}, u32[]{:S(2)}, u32[]{:S(2)}) collective-permute-start(f32[8,4096]{1,0:T(8,128)} %refs_0_.1), channel_id=1, source_target_pairs={{0,128},{64,192},{128,0},{192,64},{1,129},{65,193},{129,1},{193,65... | collective-permute-start | bytes 393224 | tf_op jit(solution)/shard_map/ppermute | solution.py:359
  1.4 11.8 %collective-permute-start = (f32[8,4096]{1,0:T(8,128)}, f32[8,4096]{1,0:T(8,128)S(1)}, u32[]{:S(2)}, u32[]{:S(2)}) collective-permute-start(f32[8,4096]{1,0:T(8,128)} %refs_0_.1), channel_id=1, source_target_pairs={{0,192},{64,0},{128,64},{192,128},{1,193},{65,1},{129,65},{193,129... | collective-permute-start | bytes 393224 | tf_op jit(solution)/shard_map/ppermute | solution.py:357
  1.4 11.8 %collective-permute-start.2 = (f32[8,4096]{1,0:T(8,128)}, f32[8,4096]{1,0:T(8,128)S(1)}, u32[]{:S(2)}, u32[]{:S(2)}) collective-permute-start(f32[8,4096]{1,0:T(8,128)} %refs_0_.1), channel_id=1, source_target_pairs={{0,64},{64,128},{128,192},{192,0},{1,65},{65,129},{129,193},{193,1... | collective-permute-start | bytes 393224 | tf_op jit(solution)/shard_map/ppermute | solution.py:356
  4.6 8.6 %copy-start = (f32[8,4096]{1,0:T(8,128)S(1)}, f32[8,4096]{1,0:T(8,128)}, u32[]{:S(2)}) copy-start(f32[8,4096]{1,0:T(8,128)} %refs_0_.1) | copy-start | bytes 393220
  4.6 10.8 %copy-start.1 = (s32[4,1,128]{2,1,0:T(1,128)S(1)}, s32[4,1,128]{2,1,0:T(1,128)}, u32[]{:S(2)}) copy-start(s32[4,1,128]{2,1,0:T(1,128)} %refs_1_.5) | copy-start | bytes 6148
  13.3 7.6 %collective-permute-start.5 = (f32[32,4096]{1,0:T(8,128)S(1)}, f32[32,4096]{1,0:T(8,128)S(1)}, u32[]{:S(2)}, u32[]{:S(2)}) collective-permute-start(f32[32,4096]{1,0:T(8,128)S(1)} %stack.1.refs_3_), channel_id=1, source_target_pairs={{0,1},{1,0},{2,3},{3,2},{4,5},{5,4},{6,7},{7,6},{8,9},{9,8},{10,11... | collective-permute-start | bytes 1572872 | tf_op jit(solution)/shard_map/ppermute | solution.py:368
  13.4 16.4 %collective-permute-start.10 = (f32[32,4096]{1,0:T(8,128)S(1)}, f32[32,4096]{1,0:T(8,128)S(1)}, u32[]{:S(2)}, u32[]{:S(2)}) collective-permute-start(f32[32,4096]{1,0:T(8,128)S(1)} %stack.1.refs_3_), channel_id=1, source_target_pairs={{1,2},{2,1},{3,4},{4,3},{5,6},{6,5},{7,8},{8,7},{9,10},{10,9},{11,... | collective-permute-start | bytes 1572872 | tf_op jit(solution)/shard_map/ppermute | solution.py:367
  18.8 8.7 %collective-permute-start.3 = (f32[2,4,64,128]{3,2,1,0:T(8,128)S(1)}, f32[2,4,64,128]{3,2,1,0:T(8,128)S(1)}, u32[]{:S(2)}, u32[]{:S(2)}) collective-permute-start(f32[2,4,64,128]{3,2,1,0:T(8,128)S(1)} %get-tuple-element.31), channel_id=1, source_target_pairs={{0,64},{64,128},{128,192},{192,0},{1,65},{65,129},{129,193},{193,1... | collective-permute-start | bytes 786440 | tf_op jit(solution)/shard_map/ppermute | solution.py:356
  19.5 10.3 %collective-permute-start.4 = (f32[2,4,64,128]{3,2,1,0:T(8,128)S(1)}, f32[2,4,64,128]{3,2,1,0:T(8,128)S(1)}, u32[]{:S(2)}, u32[]{:S(2)}) collective-permute-start(f32[2,4,64,128]{3,2,1,0:T(8,128)S(1)} %get-tuple-element.32), channel_id=1, source_target_pairs={{0,192},{64,0},{128,64},{192,128},{1,193},{65,1},{129,65},{193,129... | collective-permute-start | bytes 786440 | tf_op jit(solution)/shard_map/ppermute | solution.py:357
  23.7 11.0 %collective-permute-start.8 = (f32[2,4,64,128]{3,2,1,0:T(8,128)S(1)}, f32[2,4,64,128]{3,2,1,0:T(8,128)S(1)}, u32[]{:S(2)}, u32[]{:S(2)}) collective-permute-start(f32[2,4,64,128]{3,2,1,0:T(8,128)S(1)} %get-tuple-element.38), channel_id=1, source_target_pairs={{0,64},{64,128},{128,192},{192,0},{1,65},{65,129},{129,193},{193,1... | collective-permute-start | bytes 786440 | tf_op jit(solution)/shard_map/ppermute | solution.py:356
  25.4 10.1 %collective-permute-start.9 = (f32[2,4,64,128]{3,2,1,0:T(8,128)S(1)}, f32[2,4,64,128]{3,2,1,0:T(8,128)S(1)}, u32[]{:S(2)}, u32[]{:S(2)}) collective-permute-start(f32[2,4,64,128]{3,2,1,0:T(8,128)S(1)} %get-tuple-element.39), channel_id=1, source_target_pairs={{0,192},{64,0},{128,64},{192,128},{1,193},{65,1},{129,65},{193,129... | collective-permute-start | bytes 786440 | tf_op jit(solution)/shard_map/ppermute | solution.py:357
  32.6 9.2 %collective-permute-start.13 = (f32[2,4,64,128]{3,2,1,0:T(8,128)S(1)}, f32[2,4,64,128]{3,2,1,0:T(8,128)S(1)}, u32[]{:S(2)}, u32[]{:S(2)}) collective-permute-start(f32[2,4,64,128]{3,2,1,0:T(8,128)S(1)} %get-tuple-element.45), channel_id=1, source_target_pairs={{0,64},{64,128},{128,192},{192,0},{1,65},{65,129},{129,193},{193,1... | collective-permute-start | bytes 786440 | tf_op jit(solution)/shard_map/ppermute | solution.py:356
  32.7 10.4 %collective-permute-start.14 = (f32[2,4,64,128]{3,2,1,0:T(8,128)S(1)}, f32[2,4,64,128]{3,2,1,0:T(8,128)S(1)}, u32[]{:S(2)}, u32[]{:S(2)}) collective-permute-start(f32[2,4,64,128]{3,2,1,0:T(8,128)S(1)} %get-tuple-element.46), channel_id=1, source_target_pairs={{0,192},{64,0},{128,64},{192,128},{1,193},{65,1},{129,65},{193,129... | collective-permute-start | bytes 786440 | tf_op jit(solution)/shard_map/ppermute | solution.py:357
  35.5 9.1 %collective-permute-start.11 = (f32[1,4,64,128]{3,2,1,0:T(8,128)S(1)}, f32[1,4,64,128]{3,2,1,0:T(8,128)S(1)}, u32[]{:S(2)}, u32[]{:S(2)}) collective-permute-start(f32[1,4,64,128]{3,2,1,0:T(8,128)S(1)} %get-tuple-element.43), channel_id=1, source_target_pairs={{0,64},{64,128},{128,192},{192,0},{1,65},{65,129},{129,193},{193,1... | collective-permute-start | bytes 393224 | tf_op jit(solution)/shard_map/ppermute | solution.py:356
  36.3 11.1 %collective-permute-start.6 = (f32[1,4,64,128]{3,2,1,0:T(8,128)S(1)}, f32[1,4,64,128]{3,2,1,0:T(8,128)S(1)}, u32[]{:S(2)}, u32[]{:S(2)}) collective-permute-start(f32[1,4,64,128]{3,2,1,0:T(8,128)S(1)} %get-tuple-element.36.refs_5_), channel_id=1, source_target_pairs={{0,64},{64,128},{128,192},{192,0},{1,65},{65,129},{129,193},{193,1... | collective-permute-start | bytes 393224 | tf_op jit(solution)/shard_map/ppermute | solution.py:356
  36.4 10.4 %collective-permute-start.7 = (f32[1,4,64,128]{3,2,1,0:T(8,128)S(1)}, f32[1,4,64,128]{3,2,1,0:T(8,128)S(1)}, u32[]{:S(2)}, u32[]{:S(2)}) collective-permute-start(f32[1,4,64,128]{3,2,1,0:T(8,128)S(1)} %get-tuple-element.37), channel_id=1, source_target_pairs={{0,192},{64,0},{128,64},{192,128},{1,193},{65,1},{129,65},{193,129... | collective-permute-start | bytes 393224 | tf_op jit(solution)/shard_map/ppermute | solution.py:357
  41.8 6.2 %collective-permute-start.12 = (f32[1,4,64,128]{3,2,1,0:T(8,128)S(1)}, f32[1,4,64,128]{3,2,1,0:T(8,128)S(1)}, u32[]{:S(2)}, u32[]{:S(2)}) collective-permute-start(f32[1,4,64,128]{3,2,1,0:T(8,128)S(1)} %get-tuple-element.44), channel_id=1, source_target_pairs={{0,192},{64,0},{128,64},{192,128},{1,193},{65,1},{129,65},{193,129... | collective-permute-start | bytes 393224 | tf_op jit(solution)/shard_map/ppermute | solution.py:357
  44.7 5.0 %collective-permute-start.15 = (f32[1,4,64,128]{3,2,1,0:T(8,128)S(1)}, f32[1,4,64,128]{3,2,1,0:T(8,128)S(1)}, u32[]{:S(2)}, u32[]{:S(2)}) collective-permute-start(f32[1,4,64,128]{3,2,1,0:T(8,128)S(1)} %get-tuple-element.49), channel_id=1, source_target_pairs={{0,64},{64,128},{128,192},{192,0},{1,65},{65,129},{129,193},{193,1... | collective-permute-start | bytes 393224 | tf_op jit(solution)/shard_map/ppermute | solution.py:356
  45.9 6.2 %collective-permute-start.16 = (f32[1,4,64,128]{3,2,1,0:T(8,128)S(1)}, f32[1,4,64,128]{3,2,1,0:T(8,128)S(1)}, u32[]{:S(2)}, u32[]{:S(2)}) collective-permute-start(f32[1,4,64,128]{3,2,1,0:T(8,128)S(1)} %get-tuple-element.50), channel_id=1, source_target_pairs={{0,192},{64,0},{128,64},{192,128},{1,193},{65,1},{129,65},{193,129... | collective-permute-start | bytes 393224 | tf_op jit(solution)/shard_map/ppermute | solution.py:357

commit v3 on v2

--- a/solution.py
+++ b/solution.py
@@ -17,7 +17,7 @@
 TILES = RB * KT
 PAIRS = NPOOL // 2
 LIST = TILES + UNROLL
-GROUP = 3
+GROUP = 9
 XP = 32
 PLACES = ((0, 1), (4, 3), (5, 6), (2,), (7,))
 f32 = jnp.float32

time: 54.1 us -> 52.4 us (0.969); the launches traced: 53.1 us -> 52 us
  Pallas kernels: 18.6 us -> 18 us
    pallas_call x1, Pallas kernels: 8.54 us -> 7.08 us  [left_products(): pl.pallas_call(functools.partial(left_kernel, lax.axis_size('slab')), out...]
    ppermute x7, waiting for transfers between devices: 8.97 us -> 7.94 us  [on_device(): up = lambda x: lax.ppermute(x, 'row', ring(1))]
    pallas_call x3, Pallas kernels: 8.87 us -> 9.81 us  [right_products(): pl.pallas_call(functools.partial(right_kernel, which, sizes, len(after)),...]
    ppermute x7, starting transfers between devices: 6.82 us -> 5.98 us  [on_device(): down = lambda x: lax.ppermute(x, 'row', ring(-1))]
    ppermute x7, waiting for transfers between devices: 7.2 us -> 8.03 us  [on_device(): down = lambda x: lax.ppermute(x, 'row', ring(-1))]
where the time goes in v3:
time: 52.4 us; the launch traced here: 52 us
  Pallas kernels  18 us (34%)
  starting transfers between devices  17.9 us (34%)
  waiting for transfers between devices  16 us (31%)
    pallas_call x3, Pallas kernels, right_products(): pl.pallas_call(functools.partial(right_kernel, which, sizes, len(after)),...  9.81 us
    ppermute x7, starting transfers between devices, on_device(): up = lambda x: lax.ppermute(x, 'row', ring(1))  8.3 us
    ppermute x7, waiting for transfers between devices, on_device(): down = lambda x: lax.ppermute(x, 'row', ring(-1))  8.03 us
    ppermute x7, waiting for transfers between devices, on_device(): up = lambda x: lax.ppermute(x, 'row', ring(1))  7.94 us
    pallas_call x1, Pallas kernels, left_products(): pl.pallas_call(functools.partial(left_kernel, lax.axis_size('slab')), out...  7.08 us
    ppermute x7, starting transfers between devices, on_device(): down = lambda x: lax.ppermute(x, 'row', ring(-1))  5.98 us
    ppermute x1, starting transfers between devices, on_device(): from_other = lax.ppermute(stacked, 'slab', others)  2.11 us
    ppermute x1, starting transfers between devices, on_device(): from_far = lax.ppermute(p_tiles, 'row', ring(2))  1.41 us
  transfers between devices with their start and end apart: 17, of which 10 were waited for; matrix products, arithmetic and copies ran while one was open for 0% of the time, Pallas kernels for 33%

profile of v3, /device:TPU:86, one launch (start us, length us, event | category | flops | bytes accessed | tf_op | source)
XLA Modules:
  0.0 52.0 jit_solution(664451865980873055)
XLA Ops:
  0.0 1.4 %collective-permute-start.1 = (f32[8,4096]{1,0:T(8,128)}, f32[8,4096]{1,0:T(8,128)S(1)}, u32[]{:S(2)}, u32[]{:S(2)}) collective-permute-start(f32[8,4096]{1,0:T(8,128)} %refs_0_.1), channel_id=1, source_target_pairs={{0,128},{64,192},{128,0},{192,64},{1,129},{65,193},{129,1},{193,65... | collective-permute-start | bytes 393224 | tf_op jit(solution)/shard_map/ppermute | solution.py:359
  1.4 0.0 collective-permute-start
  1.4 3.2 %collective-permute-start.2 = (f32[8,4096]{1,0:T(8,128)}, f32[8,4096]{1,0:T(8,128)S(1)}, u32[]{:S(2)}, u32[]{:S(2)}) collective-permute-start(f32[8,4096]{1,0:T(8,128)} %refs_0_.1), channel_id=1, source_target_pairs={{0,64},{64,128},{128,192},{192,0},{1,65},{65,129},{129,193},{193,1... | collective-permute-start | bytes 393224 | tf_op jit(solution)/shard_map/ppermute | solution.py:356
  4.6 7.1 %left_products.1 = (bf16[216,64,128]{2,1,0:T(8,128)(2,1)S(1)}, s32[675]{0:T(1024)S(1)}) custom-call(f32[6912,128]{1,0:T(8,128)} %bitcast.8, f32[8,4096]{1,0:T(8,128)} %refs_0_.1, s32[8,27]{1,0:T(8,128)} %cols_hbm.1, s32[8]{0:T(128)} %counts_hbm.1, s32[4,1,128]{2,1,0:T(1,128)} %refs_1_.5, s32[1,1,8]{2,1,0:T(1,128)} %owners_hbm.1), custom_call_target="tpu_custom_call" | custom-call | flops 4000000000 | bytes 8000000 | tf_op jit(solution)/shard_map/left_products/pallas_call | solution.py:159
  11.7 0.0 collective-permute-done.1.refs_2_
  11.8 0.0 collective-permute-done.2.refs_3_
  11.8 0.1 collective-permute-start.5
  11.9 2.1 %collective-permute-start.10 = (f32[32,4096]{1,0:T(8,128)S(1)}, f32[32,4096]{1,0:T(8,128)S(1)}, u32[]{:S(2)}, u32[]{:S(2)}) collective-permute-start(f32[32,4096]{1,0:T(8,128)S(1)} %stack.1.refs_3_), channel_id=1, source_target_pairs={{1,2},{2,1},{3,4},{4,3},{5,6},{6,5},{7,8},{8,7},{9,10},{10,9},{11,... | collective-permute-start | bytes 1572872 | tf_op jit(solution)/shard_map/ppermute | solution.py:367
  14.1 3.2 %right_products.3 = (f32[2,4,64,128]{3,2,1,0:T(8,128)S(1)}, f32[2,4,64,128]{3,2,1,0:T(8,128)S(1)}, f32[2,4,64,128]{3,2,1,0:T(8,128)S(1)}, f32[1,4,64,128]{3,2,1,0:T(8,128)S(1)}, f32[1,4,64,128]{3,2,1,0:T(8,128)S(1)}) custom-call(s32[675]{0:T(1024)S(1)} %get-tuple-element.28.refs_4_.refs_0_, s32[4,1,128]{2,1,0:T(1,128)S(1)} %copy-done.1, ...), custom_call_target="tpu_custom_call" | custom-call | flops 3000000000 | bytes 5000000 | tf_op jit(solution)/shard_map/right_products/pallas_call | solution.py:261
  17.3 1.0 %collective-permute-start.3 = (f32[2,4,64,128]{3,2,1,0:T(8,128)S(1)}, f32[2,4,64,128]{3,2,1,0:T(8,128)S(1)}, u32[]{:S(2)}, u32[]{:S(2)}) collective-permute-start(f32[2,4,64,128]{3,2,1,0:T(8,128)S(1)} %get-tuple-element.31), channel_id=1, source_target_pairs={{0,64},{64,128},{128,192},{192,0},{1,65},{65,129},{129,193},{193,1... | collective-permute-start | bytes 786440 | tf_op jit(solution)/shard_map/ppermute | solution.py:356
  18.3 1.1 %collective-permute-start.4 = (f32[2,4,64,128]{3,2,1,0:T(8,128)S(1)}, f32[2,4,64,128]{3,2,1,0:T(8,128)S(1)}, u32[]{:S(2)}, u32[]{:S(2)}) collective-permute-start(f32[2,4,64,128]{3,2,1,0:T(8,128)S(1)} %get-tuple-element.32), channel_id=1, source_target_pairs={{0,192},{64,0},{128,64},{192,128},{1,193},{65,1},{129,65},{193,129... | collective-permute-start | bytes 786440 | tf_op jit(solution)/shard_map/ppermute | solution.py:357
  19.4 3.3 %right_products.4 = (f32[2,4,64,128]{3,2,1,0:T(8,128)S(1)}, f32[2,4,64,128]{3,2,1,0:T(8,128)S(1)}, f32[2,4,64,128]{3,2,1,0:T(8,128)S(1)}, f32[1,4,64,128]{3,2,1,0:T(8,128)S(1)}, f32[1,4,64,128]{3,2,1,0:T(8,128)S(1)}) custom-call(s32[675]{0:T(1024)S(1)} %get-tuple-element.28.refs_4_.refs_0_, s32[4,1,128]{2,1,0:T(1,128)S(1)} %copy-done.1, ...), custom_call_target="tpu_custom_call" | custom-call | flops 3000000000 | bytes 5000000 | tf_op jit(solution)/shard_map/right_products/pallas_call | solution.py:261
  22.7 2.3 %collective-permute-start.8 = (f32[2,4,64,128]{3,2,1,0:T(8,128)S(1)}, f32[2,4,64,128]{3,2,1,0:T(8,128)S(1)}, u32[]{:S(2)}, u32[]{:S(2)}) collective-permute-start(f32[2,4,64,128]{3,2,1,0:T(8,128)S(1)} %get-tuple-element.38), channel_id=1, source_target_pairs={{0,64},{64,128},{128,192},{192,0},{1,65},{65,129},{129,193},{193,1... | collective-permute-start | bytes 786440 | tf_op jit(solution)/shard_map/ppermute | solution.py:356
  25.0 0.9 %collective-permute-done.3.up_one.refs_1_ = f32[2,4,64,128]{3,2,1,0:T(8,128)S(1)} collective-permute-done((f32[2,4,64,128]{3,2,1,0:T(8,128)S(1)}, f32[2,4,64,128]{3,2,1,0:T(8,128)S(1)}, u32[]{:S(2)}, u32[]{:S(2)}) %collective-permute-start.3) | collective-permute-done | bytes 262176 | tf_op jit(solution)/shard_map/ppermute | solution.py:356
  26.0 2.1 %collective-permute-done.4.down_one.refs_2_ = f32[2,4,64,128]{3,2,1,0:T(8,128)S(1)} collective-permute-done((f32[2,4,64,128]{3,2,1,0:T(8,128)S(1)}, f32[2,4,64,128]{3,2,1,0:T(8,128)S(1)}, u32[]{:S(2)}, u32[]{:S(2)}) %collective-permute-start.4) | collective-permute-done | bytes 262176 | tf_op jit(solution)/shard_map/ppermute | solution.py:357
  28.2 3.3 %right_products.5 = (f32[2,4,64,128]{3,2,1,0:T(8,128)S(1)}, f32[2,4,64,128]{3,2,1,0:T(8,128)S(1)}, f32[2,4,64,128]{3,2,1,0:T(8,128)S(1)}, f32[1,4,64,128]{3,2,1,0:T(8,128)S(1)}, f32[1,4,64,128]{3,2,1,0:T(8,128)S(1)}) custom-call(s32[675]{0:T(1024)S(1)} %get-tuple-element.28.refs_4_.refs_0_, s32[4,1,128]{2,1,0:T(1,128)S(1)} %copy-done.1, ...), custom_call_target="tpu_custom_call" | custom-call | flops 3000000000 | bytes 5000000 | tf_op jit(solution)/shard_map/right_products/pallas_call | solution.py:261
  31.5 0.1 collective-permute-start.13
  31.6 2.0 %collective-permute-start.14 = (f32[2,4,64,128]{3,2,1,0:T(8,128)S(1)}, f32[2,4,64,128]{3,2,1,0:T(8,128)S(1)}, u32[]{:S(2)}, u32[]{:S(2)}) collective-permute-start(f32[2,4,64,128]{3,2,1,0:T(8,128)S(1)} %get-tuple-element.46), channel_id=1, source_target_pairs={{0,192},{64,0},{128,64},{192,128},{1,193},{65,1},{129,65},{193,129... | collective-permute-start | bytes 786440 | tf_op jit(solution)/shard_map/ppermute | solution.py:357
  33.6 1.2 %collective-permute-done.9.down_one.refs_7_ = f32[2,4,64,128]{3,2,1,0:T(8,128)S(1)} collective-permute-done((f32[2,4,64,128]{3,2,1,0:T(8,128)S(1)}, f32[2,4,64,128]{3,2,1,0:T(8,128)S(1)}, u32[]{:S(2)}, u32[]{:S(2)}) %collective-permute-start.9) | collective-permute-done | bytes 262176 | tf_op jit(solution)/shard_map/ppermute | solution.py:357
  34.9 0.4 collective-permute-start.11
  35.2 0.1 collective-permute-start.6
  35.3 1.9 %collective-permute-start.7 = (f32[1,4,64,128]{3,2,1,0:T(8,128)S(1)}, f32[1,4,64,128]{3,2,1,0:T(8,128)S(1)}, u32[]{:S(2)}, u32[]{:S(2)}) collective-permute-start(f32[1,4,64,128]{3,2,1,0:T(8,128)S(1)} %get-tuple-element.37), channel_id=1, source_target_pairs={{0,192},{64,0},{128,64},{192,128},{1,193},{65,1},{129,65},{193,129... | collective-permute-start | bytes 393224 | tf_op jit(solution)/shard_map/ppermute | solution.py:357
  37.2 3.5 %collective-permute-done.13.up_one.refs_11_ = f32[2,4,64,128]{3,2,1,0:T(8,128)S(1)} collective-permute-done((f32[2,4,64,128]{3,2,1,0:T(8,128)S(1)}, f32[2,4,64,128]{3,2,1,0:T(8,128)S(1)}, u32[]{:S(2)}, u32[]{:S(2)}) %collective-permute-start.13) | collective-permute-done | bytes 262176 | tf_op jit(solution)/shard_map/ppermute | solution.py:356
  40.8 1.5 %collective-permute-done.14.down_one.refs_12_ = f32[2,4,64,128]{3,2,1,0:T(8,128)S(1)} collective-permute-done((f32[2,4,64,128]{3,2,1,0:T(8,128)S(1)}, f32[2,4,64,128]{3,2,1,0:T(8,128)S(1)}, u32[]{:S(2)}, u32[]{:S(2)}) %collective-permute-start.14) | collective-permute-done | bytes 262176 | tf_op jit(solution)/shard_map/ppermute | solution.py:357
  42.3 1.3 %collective-permute-done.11.refs_0_.refs_8_ = f32[1,4,64,128]{3,2,1,0:T(8,128)S(1)} collective-permute-done((f32[1,4,64,128]{3,2,1,0:T(8,128)S(1)}, f32[1,4,64,128]{3,2,1,0:T(8,128)S(1)}, u32[]{:S(2)}, u32[]{:S(2)}) %collective-permute-start.11) | collective-permute-done | bytes 131104 | tf_op jit(solution)/shard_map/ppermute | solution.py:356
  43.6 1.2 %collective-permute-start.15 = (f32[1,4,64,128]{3,2,1,0:T(8,128)S(1)}, f32[1,4,64,128]{3,2,1,0:T(8,128)S(1)}, u32[]{:S(2)}, u32[]{:S(2)}) collective-permute-start(f32[1,4,64,128]{3,2,1,0:T(8,128)S(1)} %get-tuple-element.49), channel_id=1, source_target_pairs={{0,64},{64,128},{128,192},{192,0},{1,65},{65,129},{129,193},{193,1... | collective-permute-start | bytes 393224 | tf_op jit(solution)/shard_map/ppermute | solution.py:356
  44.8 0.9 %collective-permute-start.16 = (f32[1,4,64,128]{3,2,1,0:T(8,128)S(1)}, f32[1,4,64,128]{3,2,1,0:T(8,128)S(1)}, u32[]{:S(2)}, u32[]{:S(2)}) collective-permute-start(f32[1,4,64,128]{3,2,1,0:T(8,128)S(1)} %get-tuple-element.50), channel_id=1, source_target_pairs={{0,192},{64,0},{128,64},{192,128},{1,193},{65,1},{129,65},{193,129... | collective-permute-start | bytes 393224 | tf_op jit(solution)/shard_map/ppermute | solution.py:357
  45.7 0.6 %collective-permute-done.6.refs_3_ = f32[1,4,64,128]{3,2,1,0:T(8,128)S(1)} collective-permute-done((f32[1,4,64,128]{3,2,1,0:T(8,128)S(1)}, f32[1,4,64,128]{3,2,1,0:T(8,128)S(1)}, u32[]{:S(2)}, u32[]{:S(2)}) %collective-permute-start.6) | collective-permute-done | bytes 131104 | tf_op jit(solution)/shard_map/ppermute | solution.py:356
  46.3 0.8 %collective-permute-done.12.refs_9_ = f32[1,4,64,128]{3,2,1,0:T(8,128)S(1)} collective-permute-done((f32[1,4,64,128]{3,2,1,0:T(8,128)S(1)}, f32[1,4,64,128]{3,2,1,0:T(8,128)S(1)}, u32[]{:S(2)}, u32[]{:S(2)}) %collective-permute-start.12) | collective-permute-done | bytes 131104 | tf_op jit(solution)/shard_map/ppermute | solution.py:357
  47.1 1.5 %collective-permute-done.15.refs_13_ = f32[1,4,64,128]{3,2,1,0:T(8,128)S(1)} collective-permute-done((f32[1,4,64,128]{3,2,1,0:T(8,128)S(1)}, f32[1,4,64,128]{3,2,1,0:T(8,128)S(1)}, u32[]{:S(2)}, u32[]{:S(2)}) %collective-permute-start.15) | collective-permute-done | bytes 131104 | tf_op jit(solution)/shard_map/ppermute | solution.py:356
  48.7 2.4 %collective-permute-done.16.refs_14_ = f32[1,4,64,128]{3,2,1,0:T(8,128)S(1)} collective-permute-done((f32[1,4,64,128]{3,2,1,0:T(8,128)S(1)}, f32[1,4,64,128]{3,2,1,0:T(8,128)S(1)}, u32[]{:S(2)}, u32[]{:S(2)}) %collective-permute-start.16) | collective-permute-done | bytes 131104 | tf_op jit(solution)/shard_map/ppermute | solution.py:357
  51.0 1.0 %finish.1 = f32[2,64,1536]{2,1,0:T(8,128)} custom-call(f32[2,4,64,128]{3,2,1,0:T(8,128)S(1)} %get-tuple-element.30.refs_4_.refs_0_, f32[2,4,64,128]{3,2,1,0:T(8,128)S(1)} %collective-permute-done.3.up_one.refs_1_, f32[2,4,64,128]{3,2,1,0:T(8,128)S(1)} %collective-permute-done.4.down_one.refs_2_, f32[1,4,64,128]{3,2,1,0:T(8,128)S(1)} %collective-permute-done.6.refs_3_, ...), custom_call_target="tpu_custom_call" | custom-call | tf_op jit(solution)/shard_map/finish/pallas_call | solution.py:319
  (15 shorter events, 0.2 us)
Async XLA Ops:
  0.0 11.7 %collective-permute-start.1 = (f32[8,4096]{1,0:T(8,128)}, f32[8,4096]{1,0:T(8,128)S(1)}, u32[]{:S(2)}, u32[]{:S(2)}) collective-permute-start(f32[8,4096]{1,0:T(8,128)} %refs_0_.1), channel_id=1, source_target_pairs={{0,128},{64,192},{128,0},{192,64},{1,129},{65,193},{129,1},{193,65... | collective-permute-start | bytes 393224 | tf_op jit(solution)/shard_map/ppermute | solution.py:359
  1.4 10.3 %collective-permute-start = (f32[8,4096]{1,0:T(8,128)}, f32[8,4096]{1,0:T(8,128)S(1)}, u32[]{:S(2)}, u32[]{:S(2)}) collective-permute-start(f32[8,4096]{1,0:T(8,128)} %refs_0_.1), channel_id=1, source_target_pairs={{0,192},{64,0},{128,64},{192,128},{1,193},{65,1},{129,65},{193,129... | collective-permute-start | bytes 393224 | tf_op jit(solution)/shard_map/ppermute | solution.py:357
  1.4 10.4 %collective-permute-start.2 = (f32[8,4096]{1,0:T(8,128)}, f32[8,4096]{1,0:T(8,128)S(1)}, u32[]{:S(2)}, u32[]{:S(2)}) collective-permute-start(f32[8,4096]{1,0:T(8,128)} %refs_0_.1), channel_id=1, source_target_pairs={{0,64},{64,128},{128,192},{192,0},{1,65},{65,129},{129,193},{193,1... | collective-permute-start | bytes 393224 | tf_op jit(solution)/shard_map/ppermute | solution.py:356
  4.6 7.1 %copy-start = (f32[8,4096]{1,0:T(8,128)S(1)}, f32[8,4096]{1,0:T(8,128)}, u32[]{:S(2)}) copy-start(f32[8,4096]{1,0:T(8,128)} %refs_0_.1) | copy-start | bytes 393220
  4.6 9.4 %copy-start.1 = (s32[4,1,128]{2,1,0:T(1,128)S(1)}, s32[4,1,128]{2,1,0:T(1,128)}, u32[]{:S(2)}) copy-start(s32[4,1,128]{2,1,0:T(1,128)} %refs_1_.5) | copy-start | bytes 6148
  11.8 7.6 %collective-permute-start.5 = (f32[32,4096]{1,0:T(8,128)S(1)}, f32[32,4096]{1,0:T(8,128)S(1)}, u32[]{:S(2)}, u32[]{:S(2)}) collective-permute-start(f32[32,4096]{1,0:T(8,128)S(1)} %stack.1.refs_3_), channel_id=1, source_target_pairs={{0,1},{1,0},{2,3},{3,2},{4,5},{5,4},{6,7},{7,6},{8,9},{9,8},{10,11... | collective-permute-start | bytes 1572872 | tf_op jit(solution)/shard_map/ppermute | solution.py:368
  11.9 16.2 %collective-permute-start.10 = (f32[32,4096]{1,0:T(8,128)S(1)}, f32[32,4096]{1,0:T(8,128)S(1)}, u32[]{:S(2)}, u32[]{:S(2)}) collective-permute-start(f32[32,4096]{1,0:T(8,128)S(1)} %stack.1.refs_3_), channel_id=1, source_target_pairs={{1,2},{2,1},{3,4},{4,3},{5,6},{6,5},{7,8},{8,7},{9,10},{10,9},{11,... | collective-permute-start | bytes 1572872 | tf_op jit(solution)/shard_map/ppermute | solution.py:367
  17.3 8.7 %collective-permute-start.3 = (f32[2,4,64,128]{3,2,1,0:T(8,128)S(1)}, f32[2,4,64,128]{3,2,1,0:T(8,128)S(1)}, u32[]{:S(2)}, u32[]{:S(2)}) collective-permute-start(f32[2,4,64,128]{3,2,1,0:T(8,128)S(1)} %get-tuple-element.31), channel_id=1, source_target_pairs={{0,64},{64,128},{128,192},{192,0},{1,65},{65,129},{129,193},{193,1... | collective-permute-start | bytes 786440 | tf_op jit(solution)/shard_map/ppermute | solution.py:356
  18.3 9.9 %collective-permute-start.4 = (f32[2,4,64,128]{3,2,1,0:T(8,128)S(1)}, f32[2,4,64,128]{3,2,1,0:T(8,128)S(1)}, u32[]{:S(2)}, u32[]{:S(2)}) collective-permute-start(f32[2,4,64,128]{3,2,1,0:T(8,128)S(1)} %get-tuple-element.32), channel_id=1, source_target_pairs={{0,192},{64,0},{128,64},{192,128},{1,193},{65,1},{129,65},{193,129... | collective-permute-start | bytes 786440 | tf_op jit(solution)/shard_map/ppermute | solution.py:357
  22.7 10.9 %collective-permute-start.8 = (f32[2,4,64,128]{3,2,1,0:T(8,128)S(1)}, f32[2,4,64,128]{3,2,1,0:T(8,128)S(1)}, u32[]{:S(2)}, u32[]{:S(2)}) collective-permute-start(f32[2,4,64,128]{3,2,1,0:T(8,128)S(1)} %get-tuple-element.38), channel_id=1, source_target_pairs={{0,64},{64,128},{128,192},{192,0},{1,65},{65,129},{129,193},{193,1... | collective-permute-start | bytes 786440 | tf_op jit(solution)/shard_map/ppermute | solution.py:356
  25.0 9.8 %collective-permute-start.9 = (f32[2,4,64,128]{3,2,1,0:T(8,128)S(1)}, f32[2,4,64,128]{3,2,1,0:T(8,128)S(1)}, u32[]{:S(2)}, u32[]{:S(2)}) collective-permute-start(f32[2,4,64,128]{3,2,1,0:T(8,128)S(1)} %get-tuple-element.39), channel_id=1, source_target_pairs={{0,192},{64,0},{128,64},{192,128},{1,193},{65,1},{129,65},{193,129... | collective-permute-start | bytes 786440 | tf_op jit(solution)/shard_map/ppermute | solution.py:357
  31.5 9.3 %collective-permute-start.13 = (f32[2,4,64,128]{3,2,1,0:T(8,128)S(1)}, f32[2,4,64,128]{3,2,1,0:T(8,128)S(1)}, u32[]{:S(2)}, u32[]{:S(2)}) collective-permute-start(f32[2,4,64,128]{3,2,1,0:T(8,128)S(1)} %get-tuple-element.45), channel_id=1, source_target_pairs={{0,64},{64,128},{128,192},{192,0},{1,65},{65,129},{129,193},{193,1... | collective-permute-start | bytes 786440 | tf_op jit(solution)/shard_map/ppermute | solution.py:356
  31.6 10.7 %collective-permute-start.14 = (f32[2,4,64,128]{3,2,1,0:T(8,128)S(1)}, f32[2,4,64,128]{3,2,1,0:T(8,128)S(1)}, u32[]{:S(2)}, u32[]{:S(2)}) collective-permute-start(f32[2,4,64,128]{3,2,1,0:T(8,128)S(1)} %get-tuple-element.46), channel_id=1, source_target_pairs={{0,192},{64,0},{128,64},{192,128},{1,193},{65,1},{129,65},{193,129... | collective-permute-start | bytes 786440 | tf_op jit(solution)/shard_map/ppermute | solution.py:357
  34.9 8.7 %collective-permute-start.11 = (f32[1,4,64,128]{3,2,1,0:T(8,128)S(1)}, f32[1,4,64,128]{3,2,1,0:T(8,128)S(1)}, u32[]{:S(2)}, u32[]{:S(2)}) collective-permute-start(f32[1,4,64,128]{3,2,1,0:T(8,128)S(1)} %get-tuple-element.43), channel_id=1, source_target_pairs={{0,64},{64,128},{128,192},{192,0},{1,65},{65,129},{129,193},{193,1... | collective-permute-start | bytes 393224 | tf_op jit(solution)/shard_map/ppermute | solution.py:356
  35.2 11.1 %collective-permute-start.6 = (f32[1,4,64,128]{3,2,1,0:T(8,128)S(1)}, f32[1,4,64,128]{3,2,1,0:T(8,128)S(1)}, u32[]{:S(2)}, u32[]{:S(2)}) collective-permute-start(f32[1,4,64,128]{3,2,1,0:T(8,128)S(1)} %get-tuple-element.36.refs_5_), channel_id=1, source_target_pairs={{0,64},{64,128},{128,192},{192,0},{1,65},{65,129},{129,193},{193,1... | collective-permute-start | bytes 393224 | tf_op jit(solution)/shard_map/ppermute | solution.py:356
  35.3 10.4 %collective-permute-start.7 = (f32[1,4,64,128]{3,2,1,0:T(8,128)S(1)}, f32[1,4,64,128]{3,2,1,0:T(8,128)S(1)}, u32[]{:S(2)}, u32[]{:S(2)}) collective-permute-start(f32[1,4,64,128]{3,2,1,0:T(8,128)S(1)} %get-tuple-element.37), channel_id=1, source_target_pairs={{0,192},{64,0},{128,64},{192,128},{1,193},{65,1},{129,65},{193,129... | collective-permute-start | bytes 393224 | tf_op jit(solution)/shard_map/ppermute | solution.py:357
  40.8 6.3 %collective-permute-start.12 = (f32[1,4,64,128]{3,2,1,0:T(8,128)S(1)}, f32[1,4,64,128]{3,2,1,0:T(8,128)S(1)}, u32[]{:S(2)}, u32[]{:S(2)}) collective-permute-start(f32[1,4,64,128]{3,2,1,0:T(8,128)S(1)} %get-tuple-element.44), channel_id=1, source_target_pairs={{0,192},{64,0},{128,64},{192,128},{1,193},{65,1},{129,65},{193,129... | collective-permute-start | bytes 393224 | tf_op jit(solution)/shard_map/ppermute | solution.py:357
  43.6 5.0 %collective-permute-start.15 = (f32[1,4,64,128]{3,2,1,0:T(8,128)S(1)}, f32[1,4,64,128]{3,2,1,0:T(8,128)S(1)}, u32[]{:S(2)}, u32[]{:S(2)}) collective-permute-start(f32[1,4,64,128]{3,2,1,0:T(8,128)S(1)} %get-tuple-element.49), channel_id=1, source_target_pairs={{0,64},{64,128},{128,192},{192,0},{1,65},{65,129},{129,193},{193,1... | collective-permute-start | bytes 393224 | tf_op jit(solution)/shard_map/ppermute | solution.py:356
  44.8 6.2 %collective-permute-start.16 = (f32[1,4,64,128]{3,2,1,0:T(8,128)S(1)}, f32[1,4,64,128]{3,2,1,0:T(8,128)S(1)}, u32[]{:S(2)}, u32[]{:S(2)}) collective-permute-start(f32[1,4,64,128]{3,2,1,0:T(8,128)S(1)} %get-tuple-element.50), channel_id=1, source_target_pairs={{0,192},{64,0},{128,64},{192,128},{1,193},{65,1},{129,65},{193,129... | collective-permute-start | bytes 393224 | tf_op jit(solution)/shard_map/ppermute | solution.py:357
